TPU v7x, 32 devices: a whole 2x2x4 slice. The times are simulated.
32 devices in a mesh: pair: 16 (over z, x, core), slab: 2 (over y).
Axes of the slice: x: 2, y: 2, z: 4, core: 2. Of those that a mesh axis runs over, the one named last changes fastest.
Arguments:
- amps: bfloat16 [64, 256, 128], P(('pair', 'slab')), may hold values from -6 to 6
- symmetry: int32 [256], replicated, may hold values from 0 to 3
- screen: int32 [16, 16, 16], P('pair'), may hold values 0 or 1
- owner: int32 [256], replicated, may hold values from 0 to 15, as said below
- integrals: bfloat16 [16, 2048, 2048], P('pair', 'slab'), may hold values from -0.25 to 0.25
Outputs:
- residual: bfloat16 [64, 16, 16, 128], P(('pair', 'slab'))
Inputs may be any that keep to these rules, and one draw needn't show every extreme that they name: Every owner from 0 to 15 holds exactly 16 tiles.
All inputs are finite; a program needn't handle non-finite values. No bound on the sum of `screen` on one device may be relied on, other than what follows from the above.
Results may differ from a plain program's by a relative error of at most 0.001.
Values may be sent and summed in bfloat16 or wider, within the bound.
No kernel may reach another device: no remote copies, remote signals or barrier semaphores. Data moves between devices by JAX's collectives and lax.ppermute only.
A program may use at most 64 MiB of HBM per device.

v0:
```python
import jax
import jax.numpy as jnp
from jax import lax
from jax.sharding import PartitionSpec as P


def contract(operand, block_piece, mask_piece, per_owner, tile_width):
    rows_here = block_piece.shape[0]
    masked = (
        block_piece.reshape(rows_here, per_owner, tile_width) * mask_piece[:, :, None]
    ).reshape(rows_here, per_owner * tile_width)
    return jnp.dot(operand, masked, preferred_element_type=jnp.float32)


def on_device(amps, symmetry, screen, owner, integrals):
    n_pair = lax.axis_size("pair")
    local_rows, tile_count, tile_width = amps.shape
    per_owner = tile_count // n_pair
    owner_span = per_owner * tile_width
    tile_order = jnp.argsort(owner, stable=True).reshape(n_pair, per_owner)
    sorted_amps = jnp.take(amps, tile_order.reshape(-1), axis=1).reshape(
        local_rows, n_pair, owner_span
    )
    owned = lax.dynamic_index_in_dim(tile_order, lax.axis_index("pair"), 0, keepdims=False)
    labels = jnp.take(symmetry, owned)
    allowed = ((labels[:, None] == labels[None, :]) & (screen[0] == 1)).astype(jnp.bfloat16)
    mask_rows = jnp.repeat(allowed, tile_width, axis=0)
    block_rows = integrals[0]
    received = lax.all_to_all(sorted_amps, "pair", split_axis=1, concat_axis=1, tiled=True)
    flat_rows = received.reshape(local_rows * n_pair, owner_span)
    summed = contract(
        flat_rows,
        lax.all_gather(block_rows, "slab", axis=0, tiled=True),
        mask_rows,
        per_owner,
        tile_width,
    )
    product = summed.astype(jnp.bfloat16).reshape(local_rows, n_pair, owner_span)
    returned = lax.all_to_all(product, "pair", split_axis=1, concat_axis=1, tiled=True)
    return returned.reshape(local_rows, n_pair, per_owner, tile_width)


def solution(mesh):
    in_specs = (
        P(("pair", "slab"), None, None),
        P(),
        P("pair", None, None),
        P(),
        P("pair", "slab", None),
    )
    out_specs = P(("pair", "slab"), None, None, None)
    return jax.shard_map(
        on_device, mesh=mesh, in_specs=in_specs, out_specs=out_specs, check_vma=False
    )
```

profile of v0, /device:TPU:0, one launch (start us, length us, event | category | flops | bytes accessed | tf_op | source)
XLA Modules:
  0.0 151.1 jit_solution(2713174582048898298)
XLA Ops:
  6.5 0.0 copy-start
  6.5 0.0 all-gather.3.cloned.1.call-start
  6.5 0.7 all-gather.3.cloned.1.call-update
  7.3 3.8 %sort.17 = (s32[256]{0:T(256)}, s32[256]{0:T(256)S(1)}) sort(s32[256]{0:T(256)} %param.8, s32[256]{0:T(256)S(1)} %iota.4), dimensions={0}, to_apply=%region_0.0 | sort | flops 2048 | bytes 4096 | tf_op jit(solution)/shard_map/jit(argsort)/sort | solution.py:20
  11.1 0.0 copy-done
  11.1 1.3 gather_fusion
  12.4 0.1 gather.13
  12.5 0.1 broadcast_in_dim.25
  12.6 0.1 broadcast_in_dim.26
  12.7 0.9 broadcast_select_fusion
  13.6 7.4 %all-to-all-start = ((bf16[2,16,2048]{2,0,1:T(2,128)(2,1)}), bf16[2,16,2048]{2,0,1:T(2,128)(2,1)S(1)}, u32[]{:S(2)}, u32[]{:S(2)}) async-start(bf16[2,16,2048]{2,0,1:T(2,128)(2,1)} %broadcast_select_fusion), calls=%async_computation | async-start | bytes 262144 | tf_op jit(solution)/shard_map/all_to_all | solution.py:29
  21.0 0.1 reshape.78
  21.1 1.4 gather_fusion.1
  22.5 0.8 fusion.4
  23.3 5.7 %all-to-all-done = bf16[2,16,2048]{2,0,1:T(2,128)(2,1)S(1)} async-done(((bf16[2,16,2048]{2,0,1:T(2,128)(2,1)}), bf16[2,16,2048]{2,0,1:T(2,128)(2,1)S(1)}, u32[]{:S(2)}, u32[]{:S(2)}) %all-to-all-start) | async-done | bytes 131104 | tf_op jit(solution)/shard_map/all_to_all | solution.py:29
  29.0 86.7 %all-gather.3.cloned.1.call-done = bf16[1,2048,2048]{2,1,0:T(8,128)(2,1)} async-done(((bf16[1,1024,2048]{2,1,0:T(8,128)(2,1)}), bf16[1,2048,2048]{2,1,0:T(8,128)(2,1)}) %all-gather.3.cloned.1.call-update) | async-done | bytes 8388624 | tf_op jit(solution)/shard_map/all_gather | solution.py:33
  115.7 0.1 broadcast_in_dim.31
  115.7 9.0 %mul.14 = bf16[2048,16,128]{2,1,0:T(8,128)(2,1)S(1)} broadcast(bf16[2048,16]{1,0:T(8,128)(2,1)S(1)} %bitcast.41), dimensions={0,1} | broadcast | bytes 8454144 | tf_op jit(solution)/shard_map/mul | solution.py:10
  124.7 0.0 copy-done.1
  124.7 5.3 %fusion.3 = bf16[32,2048]{1,0:T(8,128)(2,1)S(1)} fusion(bf16[32,2048]{1,0:T(8,128)(2,1)S(1)} %bitcast.42, bf16[256,8,16,128]{3,2,1,0:T(8,128)(2,1)S(1)} %bitcast.40, bf16[1,2048,2048]{2,1,0:T(8,128)(2,1)S(1)} %copy-done.1), kind=kOutput, calls=%fused_computation.6 | convolution fusion | flops 272695296 | bytes 17039360 | tf_op jit(solution)/shard_map/dot_general | solution.py:12
  130.0 0.1 copy.11
  130.1 13.4 %all_to_all.10 = bf16[2,16,2048]{2,0,1:T(2,128)(2,1)S(1)} all-to-all(bf16[2,16,2048]{2,0,1:T(2,128)(2,1)S(1)} %copy.11), channel_id=1, replica_groups=mesh['pair'=16,'slab'=2] {'pair'}, dimensions={1} | all-to-all | bytes 262144 | tf_op jit(solution)/shard_map/all_to_all | solution.py:39
  143.5 0.1 reshape.80
  143.6 0.7 copy.12
  (11 shorter events, 0.1 us)
Async XLA Ops:
  6.5 4.6 %copy-start = (bf16[2,256,128]{2,1,0:T(8,128)(2,1)S(1)}, bf16[2,256,128]{2,1,0:T(8,128)(2,1)}, u32[]{:S(2)}) copy-start(bf16[2,256,128]{2,1,0:T(8,128)(2,1)} %param.5) | copy-start | bytes 393220
  6.5 109.1 %all-gather.3.cloned.1.call-start = ((), (), s32[]{:S(2)}) async-start(), calls=%async_computation.2 | async-start | bytes 12582912 | tf_op jit(solution)/shard_map/all_gather | solution.py:33
  13.6 15.3 %all-to-all-start = ((bf16[2,16,2048]{2,0,1:T(2,128)(2,1)}), bf16[2,16,2048]{2,0,1:T(2,128)(2,1)S(1)}, u32[]{:S(2)}, u32[]{:S(2)}) async-start(bf16[2,16,2048]{2,0,1:T(2,128)(2,1)} %broadcast_select_fusion), calls=%async_computation | async-start | bytes 262144 | tf_op jit(solution)/shard_map/all_to_all | solution.py:29
  115.6 9.0 %copy-start.1 = (bf16[1,2048,2048]{2,1,0:T(8,128)(2,1)S(1)}, bf16[1,2048,2048]{2,1,0:T(8,128)(2,1)}, u32[]{:S(2)}) copy-start(bf16[1,2048,2048]{2,1,0:T(8,128)(2,1)} %all-gather.3.cloned.1.call-done) | copy-start | bytes 25165828
Sparse Core Ops, SparseCore 0:
  8.9 106.7 all-gather.2
where the time goes:
time: 151 us
  waiting for transfers between devices  93 us (62%)
  between operations  13.5 us (9%)
  blocking collectives  13.4 us (9%)
  local copies, waits for them, and re-layouts  13 us (9%)
  starting transfers between devices  7.36 us (5%)
  other arithmetic  5.61 us (4%)
  matrix products  5.28 us (3%)
    all_gather x1, waiting for transfers between devices, on_device(): lax.all_gather(block_rows, 'slab', axis=0, tiled=True)  86.7 us
    all_to_all x1, blocking collectives, on_device(): lax.all_to_all(product, 'pair', split_axis=1, concat_axis=1, tiled=True)  13.4 us
    mul x1, local copies, waits for them, and re-layouts, contract(): block_piece.reshape(rows_here, per_owner, tile_width)  8.96 us
    all_to_all x1, starting transfers between devices, on_device(): lax.all_to_all(sorted_amps, 'pair', split_axis=1, concat_axis=1, tiled=True)  7.36 us
    all_to_all x1, waiting for transfers between devices, on_device(): lax.all_to_all(sorted_amps, 'pair', split_axis=1, concat_axis=1, tiled=True)  5.66 us
    dot_general x1, matrix products, contract(): return jnp.dot(operand, masked, preferred_element_type=jnp.float32)  5.28 us
    sort x1, other arithmetic, on_device(): tile_order = jnp.argsort(owner, stable=True).reshape(n_pair, per_owner)  3.84 us
  transfers between devices with their start and end apart: 2, of which 2 were waited for; matrix products, arithmetic and copies ran while one was open for 6% of the time, Pallas kernels for 0%

commit v1 on v0

v1 whole, which is shorter than its diff:
```python
import functools

import jax
import jax.numpy as jnp
from jax import lax
from jax.experimental import pallas as pl
from jax.experimental.pallas import tpu as pltpu
from jax.sharding import PartitionSpec as P

LANES = 128
CODE_MAX = 32767.0
SCALE_STEPS = 128.0
LEAST = 1e-37
VMEM_LIMIT = 48 * 1024 * 1024


def tile_places(owner_ref, owners, per_owner):
    pieces = owner_ref.shape[0]
    tiles = pieces * LANES
    rows = lax.broadcasted_iota(jnp.int32, (owners, LANES), 0)
    held = jnp.concatenate(
        [(owner_ref[j : j + 1, :] == rows).astype(jnp.float32) for j in range(pieces)], axis=1
    )
    earlier = (
        lax.broadcasted_iota(jnp.int32, (tiles, tiles), 0)
        < lax.broadcasted_iota(jnp.int32, (tiles, tiles), 1)
    ).astype(jnp.bfloat16)
    rank = jnp.dot(held.astype(jnp.bfloat16), earlier, preferred_element_type=jnp.float32)
    first = lax.broadcasted_iota(jnp.int32, (owners, tiles), 0).astype(jnp.float32) * per_owner
    return jnp.sum(held * (first + rank), axis=0, keepdims=True)


def order_kernel(owners, owner_ref, amps_ref, out_ref):
    local_rows, tiles, width = amps_ref.shape
    place = tile_places(owner_ref, owners, tiles // owners)
    rows = lax.broadcasted_iota(jnp.int32, (tiles, tiles), 0).astype(jnp.float32)
    pick = (rows == place).astype(jnp.bfloat16)
    for i in range(local_rows):
        out_ref[:, i * width : (i + 1) * width] = jnp.dot(
            pick, amps_ref[i], preferred_element_type=jnp.float32
        ).astype(out_ref.dtype)


def mask_kernel(owners, owner_ref, symmetry_ref, screen_ref, block_ref, out_ref, wide):
    step = pl.program_id(0)
    per_owner = screen_ref.shape[1]
    width, columns = block_ref.shape

    @pl.when(step == 0)
    def _():
        pieces = owner_ref.shape[0]
        tiles = pieces * LANES
        place = tile_places(owner_ref, owners, per_owner)
        first = lax.axis_index("pair") * per_owner
        rows = (lax.broadcasted_iota(jnp.int32, (per_owner, tiles), 0) + first).astype(jnp.float32)
        mine = (rows == place).astype(jnp.bfloat16)
        classes = lax.broadcasted_iota(jnp.int32, (16, LANES), 0)
        kinds = jnp.concatenate(
            [
                (symmetry_ref[j : j + 1, :] == classes).astype(jnp.float32)
                for j in range(pieces)
            ],
            axis=1,
        ).astype(jnp.bfloat16)
        across = (((1,), (1,)), ((), ()))
        labels = lax.dot_general(mine, kinds, across, preferred_element_type=jnp.float32)
        labels = labels.astype(jnp.bfloat16)
        same = lax.dot_general(labels, labels, across, preferred_element_type=jnp.float32)
        allowed = jnp.where(screen_ref[0] == 1, same, 0.0).astype(jnp.bfloat16)
        spread = (
            lax.broadcasted_iota(jnp.int32, (per_owner, columns), 1) // width
            == lax.broadcasted_iota(jnp.int32, (per_owner, columns), 0)
        ).astype(jnp.bfloat16)
        wide[...] = jnp.dot(allowed, spread, preferred_element_type=jnp.float32)

    here = lax.axis_index("slab") * pl.num_programs(0) + step
    keep = wide[pl.ds(here, 1), :].astype(block_ref.dtype)
    start = pl.multiple_of(step * width, width)
    out_ref[pl.ds(start, width), :] = block_ref[...] * keep


def partial_kernel(devices, local_rows, amps_ref, block_ref, out_ref, flat, operand):
    width = LANES
    tiles_here = block_ref.shape[0] // width
    per_owner = block_ref.shape[1] // width
    pitch = per_owner + 1
    for i in range(local_rows):
        flat[i] = amps_ref[:, i * width : (i + 1) * width].astype(jnp.float32)
        for k in range(tiles_here):
            operand[i * devices : (i + 1) * devices, k * width : (k + 1) * width] = flat[
                i, pl.ds(k, devices, stride=tiles_here), :
            ].astype(operand.dtype)
    lane = lax.broadcasted_iota(jnp.int32, (devices, width), 1)
    scales = jnp.zeros((devices, width), jnp.int32)
    for pair in range(per_owner // 2):
        summed = jnp.dot(
            operand[...],
            block_ref[:, pair * 2 * width : (pair + 1) * 2 * width],
            preferred_element_type=jnp.float32,
        )
        for half in range(2):
            tile = pair * 2 + half
            words = []
            for i in range(2):
                value = summed[i * devices : (i + 1) * devices, half * width : (half + 1) * width]
                top = jnp.maximum(jnp.max(jnp.abs(value), axis=1, keepdims=True), LEAST)
                code = jnp.ceil(jnp.log2(top) * SCALE_STEPS) + 1.0
                grain = jnp.exp2(code * (-1.0 / SCALE_STEPS)) * CODE_MAX
                words.append(
                    (jnp.floor(value * grain + 0.5).astype(jnp.int32), code.astype(jnp.int32))
                )
            (low, low_code), (high, high_code) = words
            out_ref[pl.ds(tile, devices, stride=pitch), :] = (high << 16) | (low & 0xFFFF)
            scales = jnp.where(lane == tile, (high_code << 16) | (low_code & 0xFFFF), scales)
    out_ref[pl.ds(per_owner, devices, stride=pitch), :] = scales


def total_kernel(slabs, coded_ref, out_ref):
    local_rows, owners, per_owner, width = out_ref.shape
    devices = owners * slabs
    pitch = per_owner + 1
    scales = coded_ref[pl.ds(per_owner, devices, stride=pitch), :]

    def halves(words):
        return ((words << 16) >> 16).astype(jnp.float32), (words >> 16).astype(jnp.float32)

    grains = [
        jnp.transpose(jnp.exp2(code * (1.0 / SCALE_STEPS)) * (1.0 / CODE_MAX))[:per_owner]
        for code in halves(scales)
    ]
    for owner in range(owners):
        totals = [0.0, 0.0]
        for slab in range(slabs):
            source = owner * slabs + slab
            values = halves(coded_ref[source * pitch : source * pitch + per_owner, :])
            for i in range(2):
                totals[i] = totals[i] + values[i] * grains[i][:, source : source + 1]
        for i in range(2):
            out_ref[i, owner] = totals[i].astype(out_ref.dtype)


def on_device(amps, symmetry, screen, owner, integrals):
    owners, slabs = lax.axis_size("pair"), lax.axis_size("slab")
    devices = owners * slabs
    local_rows, tiles, width = amps.shape
    per_owner = tiles // owners
    tiles_here = per_owner // slabs
    rows_here, columns = integrals.shape[1:]
    everyone = ("pair", "slab")
    owner = owner.reshape(-1, LANES)
    symmetry = symmetry.reshape(-1, LANES)
    in_vmem = pl.BlockSpec(memory_space=pltpu.VMEM)
    params = pltpu.CompilerParams(vmem_limit_bytes=VMEM_LIMIT)

    ordered = pl.pallas_call(
        functools.partial(order_kernel, owners),
        out_shape=jax.ShapeDtypeStruct((tiles, local_rows * width), amps.dtype),
        in_specs=[in_vmem, in_vmem],
        out_specs=in_vmem,
        compiler_params=params,
        name="order_amps",
    )(owner, amps)
    arrived = lax.all_to_all(
        ordered.reshape(devices, tiles_here, local_rows * width), everyone, 0, 0, tiled=True
    ).reshape(devices * tiles_here, local_rows * width)

    masked = pl.pallas_call(
        functools.partial(mask_kernel, owners),
        grid=(tiles_here,),
        out_shape=pltpu.VMEM((rows_here, columns), integrals.dtype),
        in_specs=[
            in_vmem,
            in_vmem,
            in_vmem,
            pl.BlockSpec((None, width, columns), lambda k: (0, k, 0)),
        ],
        out_specs=in_vmem,
        scratch_shapes=[pltpu.VMEM((per_owner, columns), jnp.float32)],
        compiler_params=params,
        cost_estimate=pl.CostEstimate(
            flops=rows_here * columns, bytes_accessed=4 * rows_here * columns, transcendentals=0
        ),
        name="mask_block",
    )(owner, symmetry, screen, integrals)

    pitch = per_owner + 1
    coded = pl.pallas_call(
        functools.partial(partial_kernel, devices, local_rows),
        out_shape=jax.ShapeDtypeStruct((devices * pitch, width), jnp.int32),
        in_specs=[in_vmem, in_vmem],
        out_specs=in_vmem,
        scratch_shapes=[
            pltpu.VMEM((local_rows, devices * tiles_here, width), jnp.float32),
            pltpu.VMEM((devices * local_rows, rows_here), amps.dtype),
        ],
        compiler_params=params,
        name="partial_sums",
    )(arrived, masked)
    returned = lax.all_to_all(
        coded.reshape(devices, 1, pitch * width), everyone, 0, 0, tiled=True
    ).reshape(devices * pitch, width)

    return pl.pallas_call(
        functools.partial(total_kernel, slabs),
        out_shape=jax.ShapeDtypeStruct((local_rows, owners, per_owner, width), amps.dtype),
        in_specs=[in_vmem],
        out_specs=in_vmem,
        compiler_params=params,
        name="total",
    )(returned)


def solution(mesh):
    in_specs = (
        P(("pair", "slab"), None, None),
        P(),
        P("pair", None, None),
        P(),
        P("pair", "slab", None),
    )
    out_specs = P(("pair", "slab"), None, None, None)
    return jax.shard_map(
        on_device, mesh=mesh, in_specs=in_specs, out_specs=out_specs, check_vma=False
    )
```

time: 151 us -> 40.4 us (0.27)
  waiting for transfers between devices: 93 us -> 0.01 us
  between operations: 13.5 us -> 0.05 us
  Pallas kernels: 0 us -> 8.3 us
  other arithmetic: 5.61 us -> 0 us
  matrix products: 5.28 us -> 0 us
  local copies, waits for them, and re-layouts: 13 us -> 7.75 us
  blocking collectives: 13.4 us -> 16.6 us
    all_gather x1 -> x0, waiting for transfers between devices: 86.7 us -> none  [on_device(): lax.all_gather(block_rows, 'slab', axis=0, tiled=True)]
    mul x1 -> x0, local copies, waits for them, and re-layouts: 8.96 us -> none  [contract(): block_piece.reshape(rows_here, per_owner, tile_width)]
    pallas_call x0 -> x4, Pallas kernels: none -> 8.3 us  [the longest x1 5.18 us: on_device(): pl.pallas_call(functools.partial(mask_kernel, owners), grid=(tiles_here,)...]
    unnamed x5 -> x14, local copies, waits for them, and re-layouts: 0.03 us -> 7.75 us
    all_to_all x1, waiting for transfers between devices: 5.66 us -> 0.01 us  [on_device(): lax.all_to_all(ordered.reshape(devices, tiles_here, local_rows * width),...]
    dot_general x1 -> x0, matrix products: 5.28 us -> none  [contract(): return jnp.dot(operand, masked, preferred_element_type=jnp.float32)]
    sort x1 -> x0, other arithmetic: 3.84 us -> none  [on_device(): tile_order = jnp.argsort(owner, stable=True).reshape(n_pair, per_owner)]
    all_to_all x1, blocking collectives: 13.4 us -> 16.6 us  [on_device(): lax.all_to_all(coded.reshape(devices, 1, pitch * width), everyone, 0, 0,...]
  transfers between devices with their start and end apart: 2 -> 1, of which waited for: 2 -> 0; matrix products, arithmetic and copies ran while one was open for 6% -> 0% of each run, Pallas kernels for 0% -> 13%
where the time goes in v1:
time: 40.4 us; the launch traced here: 40 us
  blocking collectives  16.6 us (41%)
  Pallas kernels  8.3 us (21%)
  local copies, waits for them, and re-layouts  7.75 us (19%)
  starting transfers between devices  7.3 us (18%)
    all_to_all x1, blocking collectives, on_device(): lax.all_to_all(coded.reshape(devices, 1, pitch * width), everyone, 0, 0,...  16.6 us
    unnamed x14, local copies, waits for them, and re-layouts  7.75 us
    all_to_all x1, starting transfers between devices, on_device(): lax.all_to_all(ordered.reshape(devices, tiles_here, local_rows * width),...  7.3 us
    pallas_call x1, Pallas kernels, on_device(): pl.pallas_call(functools.partial(mask_kernel, owners), grid=(tiles_here,)...  5.18 us
    pallas_call x1, Pallas kernels, on_device(): pl.pallas_call(functools.partial(partial_kernel, devices, local_rows), ou...  1.09 us
    pallas_call x1, Pallas kernels, on_device(): pl.pallas_call(functools.partial(order_kernel, owners), out_shape=jax.Sha...  1.03 us
    pallas_call x1, Pallas kernels, on_device(): pl.pallas_call(functools.partial(total_kernel, slabs), out_shape=jax.Shap...  0.99 us
  transfers between devices with their start and end apart: 1, of which 0 were waited for; matrix products, arithmetic and copies ran while one was open for 0% of the time, Pallas kernels for 13%

profile of v1, /device:TPU:0, one launch (start us, length us, event | category | flops | bytes accessed | tf_op | source)
XLA Modules:
  0.0 40.0 jit_solution(404557924470231871)
XLA Ops:
  0.0 0.0 copy-start.2
  0.0 0.9 %copy-done.2 = bf16[2,256,128]{2,1,0:T(8,128)(2,1)S(1)} copy-done((bf16[2,256,128]{2,1,0:T(8,128)(2,1)S(1)}, bf16[2,256,128]{2,1,0:T(8,128)(2,1)}, u32[]{:S(2)}) %copy-start.2) | copy-done | bytes 131096
  0.9 0.0 copy-start.4
  0.9 0.7 %copy-done.4 = s32[256]{0:T(256)S(1)} copy-done((s32[256]{0:T(256)S(1)}, s32[256]{0:T(256)}, u32[]{:S(2)}) %copy-start.4) | copy-done | bytes 1048
  1.6 1.0 %order_amps.1 = bf16[256,256]{1,0:T(8,128)(2,1)} custom-call(s32[2,128]{1,0:T(2,128)S(1)} %bitcast.9, bf16[2,256,128]{2,1,0:T(8,128)(2,1)S(1)} %copy-done.2), custom_call_target="tpu_custom_call" | custom-call | tf_op jit(solution)/shard_map/order_amps/pallas_call | solution.py:155
  2.6 7.3 %all-to-all-start = ((bf16[32,8,256]{2,1,0:T(8,128)(2,1)}), bf16[32,8,256]{2,1,0:T(8,128)(2,1)S(1)}, u32[]{:S(2)}, u32[]{:S(2)}) async-start(bf16[32,8,256]{2,1,0:T(8,128)(2,1)} %bitcast.1), calls=%async_computation | async-start | bytes 262144 | tf_op jit(solution)/shard_map/all_to_all | solution.py:163
  9.9 0.0 copy-start.3
  9.9 0.7 %copy-done.3 = s32[1,16,16]{2,1,0:T(8,128)S(1)} copy-done((s32[1,16,16]{2,1,0:T(8,128)S(1)}, s32[1,16,16]{2,1,0:T(8,128)}, u32[]{:S(2)}) %copy-start.3) | copy-done | bytes 1048
  10.6 0.0 copy-start.5
  10.6 0.7 %copy-done.5 = s32[256]{0:T(256)S(1)} copy-done((s32[256]{0:T(256)S(1)}, s32[256]{0:T(256)}, u32[]{:S(2)}) %copy-start.5) | copy-done | bytes 1048
  11.3 0.0 copy-start.6
  11.3 0.7 %copy-done.6 = s32[256]{0:T(256)S(1)} copy-done((s32[256]{0:T(256)S(1)}, s32[256]{0:T(256)}, u32[]{:S(2)}) %copy-start.6) | copy-done | bytes 1048
  12.0 5.2 %mask_block.1.block_ref = bf16[1024,2048]{1,0:T(8,128)(2,1)S(1)} custom-call(s32[2,128]{1,0:T(2,128)S(1)} %bitcast.10, s32[2,128]{1,0:T(2,128)S(1)} %bitcast.11, s32[1,16,16]{2,1,0:T(8,128)S(1)} %copy-done.3, bf16[1,1024,2048]{2,1,0:T(8,128)(2,1)} %block_ref.1), custom_call_target="tpu_custom_call" | custom-call | flops 2097152 | bytes 8388608 | tf_op jit(solution)/shard_map/mask_block/pallas_call | solution.py:167
  17.2 0.0 copy-start
  17.2 1.9 %copy-done = bf16[1024,2048]{1,0:T(8,128)(2,1)} copy-done((bf16[1024,2048]{1,0:T(8,128)(2,1)}, bf16[1024,2048]{1,0:T(8,128)(2,1)S(1)}, u32[]{:S(2)}) %copy-start) | copy-done | bytes 4194328
  19.1 0.0 all-to-all-done
  19.1 0.0 copy-start.1
  19.1 2.2 %copy-done.1 = bf16[1024,2048]{1,0:T(8,128)(2,1)S(1)} copy-done((bf16[1024,2048]{1,0:T(8,128)(2,1)S(1)}, bf16[1024,2048]{1,0:T(8,128)(2,1)}, u32[]{:S(2)}) %copy-start.1) | copy-done | bytes 4194328
  21.3 1.1 %partial_sums.1 = s32[544,128]{1,0:T(8,128)S(1)} custom-call(bf16[256,256]{1,0:T(8,128)(2,1)S(1)} %bitcast.8, bf16[1024,2048]{1,0:T(8,128)(2,1)S(1)} %copy-done.1), custom_call_target="tpu_custom_call" | custom-call | tf_op jit(solution)/shard_map/partial_sums/pallas_call | solution.py:187
  22.4 16.6 %all_to_all.10 = s32[32,1,2176]{2,1,0:T(1,128)S(1)} all-to-all(s32[32,1,2176]{2,1,0:T(1,128)S(1)} %bitcast.6), channel_id=1, replica_groups=mesh['pair'=16,'slab'=2] {'pair','slab'}, dimensions={0} | all-to-all | bytes 557056 | tf_op jit(solution)/shard_map/all_to_all | solution.py:199
  39.0 1.0 %total.1 = bf16[2,16,16,128]{3,2,1,0:T(8,128)(2,1)} custom-call(s32[544,128]{1,0:T(8,128)S(1)} %bitcast.7), custom_call_target="tpu_custom_call" | custom-call | tf_op jit(solution)/shard_map/total/pallas_call | solution.py:203
Async XLA Ops:
  0.0 0.9 %copy-start.2 = (bf16[2,256,128]{2,1,0:T(8,128)(2,1)S(1)}, bf16[2,256,128]{2,1,0:T(8,128)(2,1)}, u32[]{:S(2)}) copy-start(bf16[2,256,128]{2,1,0:T(8,128)(2,1)} %amps_ref.1) | copy-start | bytes 393220
  0.9 0.7 %copy-start.4 = (s32[256]{0:T(256)S(1)}, s32[256]{0:T(256)}, u32[]{:S(2)}) copy-start(s32[256]{0:T(256)} %param.8) | copy-start | bytes 3076
  2.6 16.5 %all-to-all-start = ((bf16[32,8,256]{2,1,0:T(8,128)(2,1)}), bf16[32,8,256]{2,1,0:T(8,128)(2,1)S(1)}, u32[]{:S(2)}, u32[]{:S(2)}) async-start(bf16[32,8,256]{2,1,0:T(8,128)(2,1)} %bitcast.1), calls=%async_computation | async-start | bytes 262144 | tf_op jit(solution)/shard_map/all_to_all | solution.py:163
  9.9 0.7 %copy-start.3 = (s32[1,16,16]{2,1,0:T(8,128)S(1)}, s32[1,16,16]{2,1,0:T(8,128)}, u32[]{:S(2)}) copy-start(s32[1,16,16]{2,1,0:T(8,128)} %screen_ref.1) | copy-start | bytes 3076
  10.6 0.7 %copy-start.5 = (s32[256]{0:T(256)S(1)}, s32[256]{0:T(256)}, u32[]{:S(2)}) copy-start(s32[256]{0:T(256)} %param.8) | copy-start | bytes 3076
  11.3 0.7 %copy-start.6 = (s32[256]{0:T(256)S(1)}, s32[256]{0:T(256)}, u32[]{:S(2)}) copy-start(s32[256]{0:T(256)} %param.6) | copy-start | bytes 3076
  17.2 1.9 %copy-start = (bf16[1024,2048]{1,0:T(8,128)(2,1)}, bf16[1024,2048]{1,0:T(8,128)(2,1)S(1)}, u32[]{:S(2)}) copy-start(bf16[1024,2048]{1,0:T(8,128)(2,1)S(1)} %mask_block.1.block_ref) | copy-start | bytes 12582916
  19.1 2.2 %copy-start.1 = (bf16[1024,2048]{1,0:T(8,128)(2,1)S(1)}, bf16[1024,2048]{1,0:T(8,128)(2,1)}, u32[]{:S(2)}) copy-start(bf16[1024,2048]{1,0:T(8,128)(2,1)} %copy-done) | copy-start | bytes 12582916

commit v2 on v1

--- a/solution.py
+++ b/solution.py
@@ -11,7 +11,7 @@
 CODE_MAX = 32767.0
 SCALE_STEPS = 128.0
 LEAST = 1e-37
-VMEM_LIMIT = 48 * 1024 * 1024
+RESIDENT = 3 << 20
 
 
 def tile_places(owner_ref, owners, per_owner):
@@ -30,74 +30,141 @@
     return jnp.sum(held * (first + rank), axis=0, keepdims=True)
 
 
-def order_kernel(owners, owner_ref, amps_ref, out_ref):
+def fetch(source, target, sem):
+    copy = pltpu.make_async_copy(source, target, sem)
+    copy.start()
+    return copy
+
+
+def order_kernel(owners, owner_hbm, amps_hbm, out_ref, owner_ref, amps_ref, sems):
     local_rows, tiles, width = amps_ref.shape
+    owner_copy = fetch(owner_hbm, owner_ref, sems.at[0])
+    amps_copy = fetch(amps_hbm, amps_ref, sems.at[1])
+    owner_copy.wait()
     place = tile_places(owner_ref, owners, tiles // owners)
     rows = lax.broadcasted_iota(jnp.int32, (tiles, tiles), 0).astype(jnp.float32)
     pick = (rows == place).astype(jnp.bfloat16)
+    amps_copy.wait()
     for i in range(local_rows):
         out_ref[:, i * width : (i + 1) * width] = jnp.dot(
             pick, amps_ref[i], preferred_element_type=jnp.float32
         ).astype(out_ref.dtype)
 
 
-def mask_kernel(owners, owner_ref, symmetry_ref, screen_ref, block_ref, out_ref, wide):
-    step = pl.program_id(0)
-    per_owner = screen_ref.shape[1]
-    width, columns = block_ref.shape
-
-    @pl.when(step == 0)
-    def _():
-        pieces = owner_ref.shape[0]
-        tiles = pieces * LANES
-        place = tile_places(owner_ref, owners, per_owner)
-        first = lax.axis_index("pair") * per_owner
-        rows = (lax.broadcasted_iota(jnp.int32, (per_owner, tiles), 0) + first).astype(jnp.float32)
-        mine = (rows == place).astype(jnp.bfloat16)
-        classes = lax.broadcasted_iota(jnp.int32, (16, LANES), 0)
-        kinds = jnp.concatenate(
-            [
-                (symmetry_ref[j : j + 1, :] == classes).astype(jnp.float32)
-                for j in range(pieces)
-            ],
-            axis=1,
-        ).astype(jnp.bfloat16)
-        across = (((1,), (1,)), ((), ()))
-        labels = lax.dot_general(mine, kinds, across, preferred_element_type=jnp.float32)
-        labels = labels.astype(jnp.bfloat16)
-        same = lax.dot_general(labels, labels, across, preferred_element_type=jnp.float32)
-        allowed = jnp.where(screen_ref[0] == 1, same, 0.0).astype(jnp.bfloat16)
-        spread = (
-            lax.broadcasted_iota(jnp.int32, (per_owner, columns), 1) // width
-            == lax.broadcasted_iota(jnp.int32, (per_owner, columns), 0)
-        ).astype(jnp.bfloat16)
-        wide[...] = jnp.dot(allowed, spread, preferred_element_type=jnp.float32)
-
-    here = lax.axis_index("slab") * pl.num_programs(0) + step
-    keep = wide[pl.ds(here, 1), :].astype(block_ref.dtype)
-    start = pl.multiple_of(step * width, width)
-    out_ref[pl.ds(start, width), :] = block_ref[...] * keep
-
-
-def partial_kernel(devices, local_rows, amps_ref, block_ref, out_ref, flat, operand):
+def mask_kernel(
+    owners,
+    owner_hbm,
+    symmetry_hbm,
+    screen_hbm,
+    block_hbm,
+    allowed_ref,
+    out_ref,
+    owner_ref,
+    symmetry_ref,
+    screen_ref,
+    sems,
+    block_sems,
+):
+    per_owner, columns = allowed_ref.shape
     width = LANES
-    tiles_here = block_ref.shape[0] // width
-    per_owner = block_ref.shape[1] // width
+    tiles_here = out_ref.shape[0] // width
+    kept = out_ref.shape[1]
+    small = [
+        fetch(owner_hbm, owner_ref, sems.at[0]),
+        fetch(symmetry_hbm, symmetry_ref, sems.at[1]),
+        fetch(screen_hbm, screen_ref, sems.at[2]),
+    ]
+    spans = [slice(k * width, (k + 1) * width) for k in range(tiles_here)]
+    blocks = [
+        fetch(block_hbm.at[0, rows, 0:kept], out_ref.at[rows, :], block_sems.at[k])
+        for k, rows in enumerate(spans)
+    ]
+    for copy in small:
+        copy.wait()
+    pieces = owner_ref.shape[0]
+    tiles = pieces * LANES
+    place = tile_places(owner_ref, owners, per_owner)
+    first = lax.axis_index("pair") * per_owner
+    rows = (lax.broadcasted_iota(jnp.int32, (per_owner, tiles), 0) + first).astype(jnp.float32)
+    mine = (rows == place).astype(jnp.bfloat16)
+    classes = lax.broadcasted_iota(jnp.int32, (16, LANES), 0)
+    kinds = jnp.concatenate(
+        [(symmetry_ref[j : j + 1, :] == classes).astype(jnp.float32) for j in range(pieces)],
+        axis=1,
+    ).astype(jnp.bfloat16)
+    across = (((1,), (1,)), ((), ()))
+    labels = lax.dot_general(mine, kinds, across, preferred_element_type=jnp.float32)
+    labels = labels.astype(jnp.bfloat16)
+    same = lax.dot_general(labels, labels, across, preferred_element_type=jnp.float32)
+    allowed = jnp.where(screen_ref[0] == 1, same, 0.0).astype(jnp.bfloat16)
+    spread = (
+        lax.broadcasted_iota(jnp.int32, (per_owner, columns), 1) // LANES
+        == lax.broadcasted_iota(jnp.int32, (per_owner, columns), 0)
+    ).astype(jnp.bfloat16)
+    allowed_ref[...] = jnp.dot(allowed, spread, preferred_element_type=jnp.float32)
+    first = lax.axis_index("slab") * tiles_here
+    for k, rows in enumerate(spans):
+        keep = allowed_ref[pl.ds(first + k, 1), 0:kept].astype(out_ref.dtype)
+        blocks[k].wait()
+        out_ref[rows, :] = out_ref[rows, :] * keep
+
+
+def partial_kernel(
+    devices,
+    local_rows,
+    amps_ref,
+    allowed_ref,
+    masked_ref,
+    block_hbm,
+    out_ref,
+    flat,
+    operand,
+    rest_ref,
+    sems,
+):
+    width = LANES
+    rows_here, kept = masked_ref.shape
+    tiles_here = rows_here // width
+    columns = allowed_ref.shape[1]
+    per_owner = columns // width
     pitch = per_owner + 1
+    chunk = 2 * width
+    late = {
+        start: fetch(
+            block_hbm.at[0, :, start : start + chunk],
+            rest_ref.at[:, start - kept : start - kept + chunk],
+            sems.at[n],
+        )
+        for n, start in enumerate(range(kept, columns, chunk))
+    }
     for i in range(local_rows):
         flat[i] = amps_ref[:, i * width : (i + 1) * width].astype(jnp.float32)
         for k in range(tiles_here):
             operand[i * devices : (i + 1) * devices, k * width : (k + 1) * width] = flat[
                 i, pl.ds(k, devices, stride=tiles_here), :
             ].astype(operand.dtype)
+    first = lax.axis_index("slab") * tiles_here
     lane = lax.broadcasted_iota(jnp.int32, (devices, width), 1)
     scales = jnp.zeros((devices, width), jnp.int32)
     for pair in range(per_owner // 2):
-        summed = jnp.dot(
-            operand[...],
-            block_ref[:, pair * 2 * width : (pair + 1) * 2 * width],
-            preferred_element_type=jnp.float32,
-        )
+        start = pair * chunk
+        if start < kept:
+            masked = masked_ref[:, start : start + chunk]
+        else:
+            keep = [
+                allowed_ref[pl.ds(first + k, 1), start : start + chunk].astype(rest_ref.dtype)
+                for k in range(tiles_here)
+            ]
+            late[start].wait()
+            masked = jnp.concatenate(
+                [
+                    rest_ref[k * width : (k + 1) * width, start - kept : start - kept + chunk]
+                    * keep[k]
+                    for k in range(tiles_here)
+                ],
+                axis=0,
+            )
+        summed = jnp.dot(operand[...], masked, preferred_element_type=jnp.float32)
         for half in range(2):
             tile = pair * 2 + half
             words = []
@@ -150,33 +217,48 @@
     owner = owner.reshape(-1, LANES)
     symmetry = symmetry.reshape(-1, LANES)
     in_vmem = pl.BlockSpec(memory_space=pltpu.VMEM)
-    params = pltpu.CompilerParams(vmem_limit_bytes=VMEM_LIMIT)
+    in_hbm = pl.BlockSpec(memory_space=pl.ANY)
+    dma = pltpu.SemaphoreType.DMA
+    alone = pltpu.CompilerParams(vmem_limit_bytes=60 << 20)
+    beside = pltpu.CompilerParams(vmem_limit_bytes=48 << 20)
+    small = pltpu.CompilerParams(vmem_limit_bytes=16 << 20)
+    chunk = 2 * width
+    kept = min(columns, RESIDENT // (rows_here * integrals.dtype.itemsize) // chunk * chunk)
+    rest = max(columns - kept, chunk)
 
     ordered = pl.pallas_call(
         functools.partial(order_kernel, owners),
         out_shape=jax.ShapeDtypeStruct((tiles, local_rows * width), amps.dtype),
-        in_specs=[in_vmem, in_vmem],
+        in_specs=[in_hbm, in_hbm],
         out_specs=in_vmem,
-        compiler_params=params,
+        scratch_shapes=[
+            pltpu.VMEM(owner.shape, owner.dtype),
+            pltpu.VMEM(amps.shape, amps.dtype),
+            dma((2,)),
+        ],
+        compiler_params=alone,
         name="order_amps",
     )(owner, amps)
     arrived = lax.all_to_all(
         ordered.reshape(devices, tiles_here, local_rows * width), everyone, 0, 0, tiled=True
     ).reshape(devices * tiles_here, local_rows * width)
 
-    masked = pl.pallas_call(
+    allowed, masked = pl.pallas_call(
         functools.partial(mask_kernel, owners),
-        grid=(tiles_here,),
-        out_shape=pltpu.VMEM((rows_here, columns), integrals.dtype),
-        in_specs=[
-            in_vmem,
-            in_vmem,
-            in_vmem,
-            pl.BlockSpec((None, width, columns), lambda k: (0, k, 0)),
+        out_shape=(
+            pltpu.VMEM((per_owner, columns), jnp.float32),
+            pltpu.VMEM((rows_here, kept), integrals.dtype),
+        ),
+        in_specs=[in_hbm] * 4,
+        out_specs=(in_vmem, in_vmem),
+        scratch_shapes=[
+            pltpu.VMEM(owner.shape, owner.dtype),
+            pltpu.VMEM(symmetry.shape, symmetry.dtype),
+            pltpu.VMEM(screen.shape, screen.dtype),
+            dma((3,)),
+            dma((tiles_here,)),
         ],
-        out_specs=in_vmem,
-        scratch_shapes=[pltpu.VMEM((per_owner, columns), jnp.float32)],
-        compiler_params=params,
+        compiler_params=beside,
         cost_estimate=pl.CostEstimate(
             flops=rows_here * columns, bytes_accessed=4 * rows_here * columns, transcendentals=0
         ),
@@ -187,15 +269,17 @@
     coded = pl.pallas_call(
         functools.partial(partial_kernel, devices, local_rows),
         out_shape=jax.ShapeDtypeStruct((devices * pitch, width), jnp.int32),
-        in_specs=[in_vmem, in_vmem],
+        in_specs=[in_vmem, in_vmem, in_vmem, in_hbm],
         out_specs=in_vmem,
         scratch_shapes=[
             pltpu.VMEM((local_rows, devices * tiles_here, width), jnp.float32),
             pltpu.VMEM((devices * local_rows, rows_here), amps.dtype),
+            pltpu.VMEM((rows_here, rest), integrals.dtype),
+            dma((rest // chunk,)),
         ],
-        compiler_params=params,
+        compiler_params=beside,
         name="partial_sums",
-    )(arrived, masked)
+    )(arrived, allowed, masked, integrals)
     returned = lax.all_to_all(
         coded.reshape(devices, 1, pitch * width), everyone, 0, 0, tiled=True
     ).reshape(devices * pitch, width)
@@ -205,7 +289,7 @@
         out_shape=jax.ShapeDtypeStruct((local_rows, owners, per_owner, width), amps.dtype),
         in_specs=[in_vmem],
         out_specs=in_vmem,
-        compiler_params=params,
+        compiler_params=small,
         name="total",
     )(returned)
 

time: 40.4 us -> 33.8 us (0.84)
  local copies, waits for them, and re-layouts: 7.75 us -> 2.05 us
  waiting for transfers between devices: 0.01 us -> 4.6 us
  blocking collectives: 16.6 us -> 12.7 us
  Pallas kernels: 8.3 us -> 6.81 us
    unnamed x14 -> x6, local copies, waits for them, and re-layouts: 7.75 us -> 2.05 us
    all_to_all x1, waiting for transfers between devices: 0.01 us -> 4.6 us  [on_device(): lax.all_to_all(ordered.reshape(devices, tiles_here, local_rows * width),...]
    all_to_all x1, blocking collectives: 16.6 us -> 12.7 us  [on_device(): lax.all_to_all(coded.reshape(devices, 1, pitch * width), everyone, 0, 0,...]
    pallas_call x1, Pallas kernels: 5.18 us -> 1.95 us  [on_device(): pl.pallas_call(functools.partial(mask_kernel, owners), out_shape=(pltpu.V...]
    pallas_call x1, Pallas kernels: 1.09 us -> 2.04 us  [on_device(): pl.pallas_call(functools.partial(partial_kernel, devices, local_rows), ou...]
    pallas_call x1, Pallas kernels: 1.03 us -> 1.82 us  [on_device(): pl.pallas_call(functools.partial(order_kernel, owners), out_shape=jax.Sha...]
  transfers between devices with their start and end apart: 1 -> 1, of which waited for: 0 -> 1; matrix products, arithmetic and copies ran while one was open for 0% -> 0% of each run, Pallas kernels for 13% -> 6%
where the time goes in v2:
time: 33.8 us; the launch traced here: 33.5 us
  blocking collectives  12.7 us (38%)
  starting transfers between devices  7.3 us (22%)
  Pallas kernels  6.81 us (20%)
  waiting for transfers between devices  4.6 us (14%)
  local copies, waits for them, and re-layouts  2.05 us (6%)
    all_to_all x1, blocking collectives, on_device(): lax.all_to_all(coded.reshape(devices, 1, pitch * width), everyone, 0, 0,...  12.7 us
    all_to_all x1, starting transfers between devices, on_device(): lax.all_to_all(ordered.reshape(devices, tiles_here, local_rows * width),...  7.3 us
    all_to_all x1, waiting for transfers between devices, on_device(): lax.all_to_all(ordered.reshape(devices, tiles_here, local_rows * width),...  4.6 us
    unnamed x6, local copies, waits for them, and re-layouts  2.05 us
    pallas_call x1, Pallas kernels, on_device(): pl.pallas_call(functools.partial(partial_kernel, devices, local_rows), ou...  2.04 us
    pallas_call x1, Pallas kernels, on_device(): pl.pallas_call(functools.partial(mask_kernel, owners), out_shape=(pltpu.V...  1.95 us
    pallas_call x1, Pallas kernels, on_device(): pl.pallas_call(functools.partial(order_kernel, owners), out_shape=jax.Sha...  1.82 us
    pallas_call x1, Pallas kernels, on_device(): pl.pallas_call(functools.partial(total_kernel, slabs), out_shape=jax.Shap...  0.99 us
  transfers between devices with their start and end apart: 1, of which 1 were waited for; matrix products, arithmetic and copies ran while one was open for 0% of the time, Pallas kernels for 6%

profile of v2, /device:TPU:0, one launch (start us, length us, event | category | flops | bytes accessed | tf_op | source)
XLA Modules:
  0.0 33.5 jit_solution(12335859133025818984)
XLA Ops:
  0.0 1.8 %order_amps.1 = bf16[256,256]{1,0:T(8,128)(2,1)} custom-call(s32[2,128]{1,0:T(2,128)} %bitcast.9, bf16[2,256,128]{2,1,0:T(8,128)(2,1)} %amps_hbm.1), custom_call_target="tpu_custom_call" | custom-call | tf_op jit(solution)/shard_map/order_amps/pallas_call | solution.py:229
  1.8 7.3 %all-to-all-start = ((bf16[32,8,256]{2,1,0:T(8,128)(2,1)}), bf16[32,8,256]{2,1,0:T(8,128)(2,1)S(1)}, u32[]{:S(2)}, u32[]{:S(2)}) async-start(bf16[32,8,256]{2,1,0:T(8,128)(2,1)} %bitcast.12), calls=%async_computation | async-start | bytes 262144 | tf_op jit(solution)/shard_map/all_to_all | solution.py:242
  9.1 0.0 copy-start
  9.2 0.7 %copy-done = s32[1,16,16]{2,1,0:T(8,128)S(1)} copy-done((s32[1,16,16]{2,1,0:T(8,128)S(1)}, s32[1,16,16]{2,1,0:T(8,128)}, u32[]{:S(2)}) %copy-start) | copy-done | bytes 1048
  9.8 0.0 copy-start.1
  9.8 0.7 %copy-done.1 = s32[256]{0:T(256)S(1)} copy-done((s32[256]{0:T(256)S(1)}, s32[256]{0:T(256)}, u32[]{:S(2)}) %copy-start.1) | copy-done | bytes 1048
  10.5 0.0 copy-start.2
  10.5 0.7 %copy-done.2 = s32[256]{0:T(256)S(1)} copy-done((s32[256]{0:T(256)S(1)}, s32[256]{0:T(256)}, u32[]{:S(2)}) %copy-start.2) | copy-done | bytes 1048
  11.2 2.0 %mask_block.1 = (f32[16,2048]{1,0:T(8,128)S(1)}, bf16[1024,1536]{1,0:T(8,128)(2,1)S(1)}) custom-call(s32[2,128]{1,0:T(2,128)S(1)} %bitcast.10, s32[2,128]{1,0:T(2,128)S(1)} %bitcast.11, s32[1,16,16]{2,1,0:T(8,128)S(1)} %copy-done, bf16[1,1024,2048]{2,1,0:T(8,128)(2,1)} %block_hbm.3), custom_call_target="tpu_custom_call" | custom-call | flops 2097152 | bytes 8388608 | tf_op jit(solution)/shard_map/mask_block/pallas_call | solution.py:246
  13.2 4.6 %all-to-all-done = bf16[32,8,256]{2,1,0:T(8,128)(2,1)S(1)} async-done(((bf16[32,8,256]{2,1,0:T(8,128)(2,1)}), bf16[32,8,256]{2,1,0:T(8,128)(2,1)S(1)}, u32[]{:S(2)}, u32[]{:S(2)}) %all-to-all-start) | async-done | bytes 131104 | tf_op jit(solution)/shard_map/all_to_all | solution.py:242
  17.8 2.0 %partial_sums.1 = s32[544,128]{1,0:T(8,128)S(1)} custom-call(bf16[256,256]{1,0:T(8,128)(2,1)S(1)} %bitcast.8, f32[16,2048]{1,0:T(8,128)S(1)} %get-tuple-element.7.allowed_ref, bf16[1024,1536]{1,0:T(8,128)(2,1)S(1)} %get-tuple-element.8.masked_ref, bf16[1,1024,2048]{2,1,0:T(8,128)(2,1)} %block_hbm.3), custom_call_target="tpu_custom_call" | custom-call | tf_op jit(solution)/shard_map/partial_sums/pallas_call | solution.py:269
  19.8 12.7 %all_to_all.10 = s32[32,1,2176]{2,1,0:T(1,128)S(1)} all-to-all(s32[32,1,2176]{2,1,0:T(1,128)S(1)} %bitcast.6), channel_id=1, replica_groups=mesh['pair'=16,'slab'=2] {'pair','slab'}, dimensions={0} | all-to-all | bytes 557056 | tf_op jit(solution)/shard_map/all_to_all | solution.py:283
  32.5 1.0 %total.1 = bf16[2,16,16,128]{3,2,1,0:T(8,128)(2,1)} custom-call(s32[544,128]{1,0:T(8,128)S(1)} %bitcast.7), custom_call_target="tpu_custom_call" | custom-call | tf_op jit(solution)/shard_map/total/pallas_call | solution.py:287
Async XLA Ops:
  1.8 15.9 %all-to-all-start = ((bf16[32,8,256]{2,1,0:T(8,128)(2,1)}), bf16[32,8,256]{2,1,0:T(8,128)(2,1)S(1)}, u32[]{:S(2)}, u32[]{:S(2)}) async-start(bf16[32,8,256]{2,1,0:T(8,128)(2,1)} %bitcast.12), calls=%async_computation | async-start | bytes 262144 | tf_op jit(solution)/shard_map/all_to_all | solution.py:242
  9.1 0.7 %copy-start = (s32[1,16,16]{2,1,0:T(8,128)S(1)}, s32[1,16,16]{2,1,0:T(8,128)}, u32[]{:S(2)}) copy-start(s32[1,16,16]{2,1,0:T(8,128)} %screen_hbm.1) | copy-start | bytes 3076
  9.8 0.7 %copy-start.1 = (s32[256]{0:T(256)S(1)}, s32[256]{0:T(256)}, u32[]{:S(2)}) copy-start(s32[256]{0:T(256)} %param.8) | copy-start | bytes 3076
  10.5 0.7 %copy-start.2 = (s32[256]{0:T(256)S(1)}, s32[256]{0:T(256)}, u32[]{:S(2)}) copy-start(s32[256]{0:T(256)} %param.6) | copy-start | bytes 3076

commit v3 on v2

--- a/solution.py
+++ b/solution.py
@@ -11,7 +11,7 @@
 CODE_MAX = 32767.0
 SCALE_STEPS = 128.0
 LEAST = 1e-37
-RESIDENT = 3 << 20
+RESIDENT = 13 << 18
 
 
 def tile_places(owner_ref, owners, per_owner):
@@ -57,15 +57,16 @@
     symmetry_hbm,
     screen_hbm,
     block_hbm,
-    allowed_ref,
+    rest_ref,
     out_ref,
     owner_ref,
     symmetry_ref,
     screen_ref,
+    wide,
     sems,
     block_sems,
 ):
-    per_owner, columns = allowed_ref.shape
+    per_owner, columns = wide.shape
     width = LANES
     tiles_here = out_ref.shape[0] // width
     kept = out_ref.shape[1]
@@ -101,10 +102,12 @@
         lax.broadcasted_iota(jnp.int32, (per_owner, columns), 1) // LANES
         == lax.broadcasted_iota(jnp.int32, (per_owner, columns), 0)
     ).astype(jnp.bfloat16)
-    allowed_ref[...] = jnp.dot(allowed, spread, preferred_element_type=jnp.float32)
+    wide[...] = jnp.dot(allowed, spread, preferred_element_type=jnp.float32)
     first = lax.axis_index("slab") * tiles_here
+    for k in range(tiles_here):
+        rest_ref[k : k + 1, :] = wide[pl.ds(first + k, 1), columns - rest_ref.shape[1] :]
     for k, rows in enumerate(spans):
-        keep = allowed_ref[pl.ds(first + k, 1), 0:kept].astype(out_ref.dtype)
+        keep = wide[pl.ds(first + k, 1), 0:kept].astype(out_ref.dtype)
         blocks[k].wait()
         out_ref[rows, :] = out_ref[rows, :] * keep
 
@@ -120,69 +123,65 @@
     flat,
     operand,
     rest_ref,
-    sems,
+    sums,
+    sem,
 ):
     width = LANES
     rows_here, kept = masked_ref.shape
     tiles_here = rows_here // width
-    columns = allowed_ref.shape[1]
+    columns = block_hbm.shape[2]
     per_owner = columns // width
     pitch = per_owner + 1
-    chunk = 2 * width
-    late = {
-        start: fetch(
-            block_hbm.at[0, :, start : start + chunk],
-            rest_ref.at[:, start - kept : start - kept + chunk],
-            sems.at[n],
-        )
-        for n, start in enumerate(range(kept, columns, chunk))
-    }
+    late = fetch(block_hbm.at[0, :, kept:columns], rest_ref, sem) if kept < columns else None
     for i in range(local_rows):
         flat[i] = amps_ref[:, i * width : (i + 1) * width].astype(jnp.float32)
         for k in range(tiles_here):
             operand[i * devices : (i + 1) * devices, k * width : (k + 1) * width] = flat[
                 i, pl.ds(k, devices, stride=tiles_here), :
             ].astype(operand.dtype)
-    first = lax.axis_index("slab") * tiles_here
-    lane = lax.broadcasted_iota(jnp.int32, (devices, width), 1)
-    scales = jnp.zeros((devices, width), jnp.int32)
+
+    def column_tile(tile):
+        start = tile * width
+        if start < kept:
+            return masked_ref[:, start : start + width]
+        return jnp.concatenate(
+            [
+                rest_ref[k * width : (k + 1) * width, start - kept : start - kept + width]
+                * allowed_ref[k : k + 1, start - kept : start - kept + width].astype(rest_ref.dtype)
+                for k in range(tiles_here)
+            ],
+            axis=0,
+        )
+
+    top = jnp.full((local_rows * devices, width), LEAST, jnp.float32)
     for pair in range(per_owner // 2):
-        start = pair * chunk
-        if start < kept:
-            masked = masked_ref[:, start : start + chunk]
+        start = pair * 2 * width
+        if start + 2 * width <= kept:
+            columns_here = masked_ref[:, start : start + 2 * width]
         else:
-            keep = [
-                allowed_ref[pl.ds(first + k, 1), start : start + chunk].astype(rest_ref.dtype)
-                for k in range(tiles_here)
-            ]
-            late[start].wait()
-            masked = jnp.concatenate(
-                [
-                    rest_ref[k * width : (k + 1) * width, start - kept : start - kept + chunk]
-                    * keep[k]
-                    for k in range(tiles_here)
-                ],
-                axis=0,
-            )
-        summed = jnp.dot(operand[...], masked, preferred_element_type=jnp.float32)
+            if late is not None:
+                late.wait()
+                late = None
+            columns_here = jnp.concatenate([column_tile(pair * 2), column_tile(pair * 2 + 1)], axis=1)
+        summed = jnp.dot(operand[...], columns_here, preferred_element_type=jnp.float32)
+        sums[:, start : start + 2 * width] = summed
         for half in range(2):
-            tile = pair * 2 + half
-            words = []
-            for i in range(2):
-                value = summed[i * devices : (i + 1) * devices, half * width : (half + 1) * width]
-                top = jnp.maximum(jnp.max(jnp.abs(value), axis=1, keepdims=True), LEAST)
-                code = jnp.ceil(jnp.log2(top) * SCALE_STEPS) + 1.0
-                grain = jnp.exp2(code * (-1.0 / SCALE_STEPS)) * CODE_MAX
-                words.append(
-                    (jnp.floor(value * grain + 0.5).astype(jnp.int32), code.astype(jnp.int32))
-                )
-            (low, low_code), (high, high_code) = words
-            out_ref[pl.ds(tile, devices, stride=pitch), :] = (high << 16) | (low & 0xFFFF)
-            scales = jnp.where(lane == tile, (high_code << 16) | (low_code & 0xFFFF), scales)
-    out_ref[pl.ds(per_owner, devices, stride=pitch), :] = scales
-
-
-def total_kernel(slabs, coded_ref, out_ref):
+            top = jnp.maximum(top, jnp.abs(summed[:, half * width : (half + 1) * width]))
+    code = jnp.ceil(jnp.log2(top) * SCALE_STEPS) + 1.0
+    grain = jnp.exp2(code * (-1.0 / SCALE_STEPS)) * CODE_MAX
+
+    def pack(words):
+        return (words[devices:] << 16) | (words[:devices] & 0xFFFF)
+
+    out_ref[pl.ds(per_owner, devices, stride=pitch), :] = pack(code.astype(jnp.int32))
+    for tile in range(per_owner):
+        value = sums[:, tile * width : (tile + 1) * width]
+        out_ref[pl.ds(tile, devices, stride=pitch), :] = pack(
+            jnp.floor(value * grain + 0.5).astype(jnp.int32)
+        )
+
+
+def total_kernel(slabs, coded_ref, out_hbm, out_ref, sems):
     local_rows, owners, per_owner, width = out_ref.shape
     devices = owners * slabs
     pitch = per_owner + 1
@@ -192,18 +191,24 @@
         return ((words << 16) >> 16).astype(jnp.float32), (words >> 16).astype(jnp.float32)
 
     grains = [
-        jnp.transpose(jnp.exp2(code * (1.0 / SCALE_STEPS)) * (1.0 / CODE_MAX))[:per_owner]
-        for code in halves(scales)
+        jnp.exp2(code * (1.0 / SCALE_STEPS)) * (1.0 / CODE_MAX) for code in halves(scales)
     ]
+    copies = []
+    group = owners // sems.shape[0]
     for owner in range(owners):
         totals = [0.0, 0.0]
         for slab in range(slabs):
             source = owner * slabs + slab
             values = halves(coded_ref[source * pitch : source * pitch + per_owner, :])
             for i in range(2):
-                totals[i] = totals[i] + values[i] * grains[i][:, source : source + 1]
+                totals[i] = totals[i] + values[i] * grains[i][source : source + 1, :]
         for i in range(2):
             out_ref[i, owner] = totals[i].astype(out_ref.dtype)
+        if (owner + 1) % group == 0:
+            done = slice(owner + 1 - group, owner + 1)
+            copies.append(fetch(out_ref.at[:, done], out_hbm.at[:, done], sems.at[owner // group]))
+    for copy in copies:
+        copy.wait()
 
 
 def on_device(amps, symmetry, screen, owner, integrals):
@@ -222,9 +227,8 @@
     alone = pltpu.CompilerParams(vmem_limit_bytes=60 << 20)
     beside = pltpu.CompilerParams(vmem_limit_bytes=48 << 20)
     small = pltpu.CompilerParams(vmem_limit_bytes=16 << 20)
-    chunk = 2 * width
-    kept = min(columns, RESIDENT // (rows_here * integrals.dtype.itemsize) // chunk * chunk)
-    rest = max(columns - kept, chunk)
+    kept = min(columns, RESIDENT // (rows_here * integrals.dtype.itemsize) // width * width)
+    rest = max(columns - kept, 2 * width)
 
     ordered = pl.pallas_call(
         functools.partial(order_kernel, owners),
@@ -246,7 +250,7 @@
     allowed, masked = pl.pallas_call(
         functools.partial(mask_kernel, owners),
         out_shape=(
-            pltpu.VMEM((per_owner, columns), jnp.float32),
+            pltpu.VMEM((tiles_here, rest), jnp.float32),
             pltpu.VMEM((rows_here, kept), integrals.dtype),
         ),
         in_specs=[in_hbm] * 4,
@@ -255,6 +259,7 @@
             pltpu.VMEM(owner.shape, owner.dtype),
             pltpu.VMEM(symmetry.shape, symmetry.dtype),
             pltpu.VMEM(screen.shape, screen.dtype),
+            pltpu.VMEM((per_owner, columns), jnp.float32),
             dma((3,)),
             dma((tiles_here,)),
         ],
@@ -275,7 +280,8 @@
             pltpu.VMEM((local_rows, devices * tiles_here, width), jnp.float32),
             pltpu.VMEM((devices * local_rows, rows_here), amps.dtype),
             pltpu.VMEM((rows_here, rest), integrals.dtype),
-            dma((rest // chunk,)),
+            pltpu.VMEM((devices * local_rows, columns), jnp.float32),
+            dma,
         ],
         compiler_params=beside,
         name="partial_sums",
@@ -288,7 +294,11 @@
         functools.partial(total_kernel, slabs),
         out_shape=jax.ShapeDtypeStruct((local_rows, owners, per_owner, width), amps.dtype),
         in_specs=[in_vmem],
-        out_specs=in_vmem,
+        out_specs=in_hbm,
+        scratch_shapes=[
+            pltpu.VMEM((local_rows, owners, per_owner, width), amps.dtype),
+            dma((4,)),
+        ],
         compiler_params=small,
         name="total",
     )(returned)

time: 33.8 us -> 33.1 us (0.979)
  Pallas kernels: 6.81 us -> 6.2 us
    pallas_call x1, Pallas kernels: 2.04 us -> 1.6 us  [on_device(): pl.pallas_call(functools.partial(partial_kernel, devices, local_rows), ou...]
where the time goes in v3:
time: 33.1 us; the launch traced here: 32.8 us
  blocking collectives  12.7 us (38%)
  starting transfers between devices  7.3 us (22%)
  Pallas kernels  6.2 us (19%)
  waiting for transfers between devices  4.52 us (14%)
  local copies, waits for them, and re-layouts  2.05 us (6%)
    all_to_all x1, blocking collectives, on_device(): lax.all_to_all(coded.reshape(devices, 1, pitch * width), everyone, 0, 0,...  12.7 us
    all_to_all x1, starting transfers between devices, on_device(): lax.all_to_all(ordered.reshape(devices, tiles_here, local_rows * width),...  7.3 us
    all_to_all x1, waiting for transfers between devices, on_device(): lax.all_to_all(ordered.reshape(devices, tiles_here, local_rows * width),...  4.52 us
    unnamed x6, local copies, waits for them, and re-layouts  2.05 us
    pallas_call x1, Pallas kernels, on_device(): pl.pallas_call(functools.partial(mask_kernel, owners), out_shape=(pltpu.V...  2.04 us
    pallas_call x1, Pallas kernels, on_device(): pl.pallas_call(functools.partial(order_kernel, owners), out_shape=jax.Sha...  1.82 us
    pallas_call x1, Pallas kernels, on_device(): pl.pallas_call(functools.partial(partial_kernel, devices, local_rows), ou...  1.6 us
    pallas_call x1, Pallas kernels, on_device(): pl.pallas_call(functools.partial(total_kernel, slabs), out_shape=jax.Shap...  0.74 us
  transfers between devices with their start and end apart: 1, of which 1 were waited for; matrix products, arithmetic and copies ran while one was open for 0% of the time, Pallas kernels for 6%

profile of v3, /device:TPU:0, one launch (start us, length us, event | category | flops | bytes accessed | tf_op | source)
XLA Modules:
  0.0 32.8 jit_solution(10454509757874732002)
XLA Ops:
  0.0 1.8 %order_amps.1 = bf16[256,256]{1,0:T(8,128)(2,1)} custom-call(s32[2,128]{1,0:T(2,128)} %bitcast.9, bf16[2,256,128]{2,1,0:T(8,128)(2,1)} %amps_hbm.1), custom_call_target="tpu_custom_call" | custom-call | tf_op jit(solution)/shard_map/order_amps/pallas_call | solution.py:233
  1.8 7.3 %all-to-all-start = ((bf16[32,8,256]{2,1,0:T(8,128)(2,1)}), bf16[32,8,256]{2,1,0:T(8,128)(2,1)S(1)}, u32[]{:S(2)}, u32[]{:S(2)}) async-start(bf16[32,8,256]{2,1,0:T(8,128)(2,1)} %bitcast.12), calls=%async_computation | async-start | bytes 262144 | tf_op jit(solution)/shard_map/all_to_all | solution.py:246
  9.1 0.0 copy-start
  9.2 0.7 %copy-done = s32[1,16,16]{2,1,0:T(8,128)S(1)} copy-done((s32[1,16,16]{2,1,0:T(8,128)S(1)}, s32[1,16,16]{2,1,0:T(8,128)}, u32[]{:S(2)}) %copy-start) | copy-done | bytes 1048
  9.8 0.0 copy-start.1
  9.8 0.7 %copy-done.1 = s32[256]{0:T(256)S(1)} copy-done((s32[256]{0:T(256)S(1)}, s32[256]{0:T(256)}, u32[]{:S(2)}) %copy-start.1) | copy-done | bytes 1048
  10.5 0.0 copy-start.2
  10.5 0.7 %copy-done.2 = s32[256]{0:T(256)S(1)} copy-done((s32[256]{0:T(256)S(1)}, s32[256]{0:T(256)}, u32[]{:S(2)}) %copy-start.2) | copy-done | bytes 1048
  11.2 2.0 %mask_block.1 = (f32[8,384]{1,0:T(8,128)S(1)}, bf16[1024,1664]{1,0:T(8,128)(2,1)S(1)}) custom-call(s32[2,128]{1,0:T(2,128)S(1)} %bitcast.10, s32[2,128]{1,0:T(2,128)S(1)} %bitcast.11, s32[1,16,16]{2,1,0:T(8,128)S(1)} %copy-done, bf16[1,1024,2048]{2,1,0:T(8,128)(2,1)} %block_hbm.3), custom_call_target="tpu_custom_call" | custom-call | flops 2097152 | bytes 8388608 | tf_op jit(solution)/shard_map/mask_block/pallas_call | solution.py:250
  13.2 4.5 %all-to-all-done = bf16[32,8,256]{2,1,0:T(8,128)(2,1)S(1)} async-done(((bf16[32,8,256]{2,1,0:T(8,128)(2,1)}), bf16[32,8,256]{2,1,0:T(8,128)(2,1)S(1)}, u32[]{:S(2)}, u32[]{:S(2)}) %all-to-all-start) | async-done | bytes 131104 | tf_op jit(solution)/shard_map/all_to_all | solution.py:246
  17.8 1.6 %partial_sums.1 = s32[544,128]{1,0:T(8,128)S(1)} custom-call(bf16[256,256]{1,0:T(8,128)(2,1)S(1)} %bitcast.8, f32[8,384]{1,0:T(8,128)S(1)} %get-tuple-element.7.allowed_ref, bf16[1024,1664]{1,0:T(8,128)(2,1)S(1)} %get-tuple-element.8.masked_ref, bf16[1,1024,2048]{2,1,0:T(8,128)(2,1)} %block_hbm.3), custom_call_target="tpu_custom_call" | custom-call | tf_op jit(solution)/shard_map/partial_sums/pallas_call | solution.py:274
  19.4 12.7 %all_to_all.10 = s32[32,1,2176]{2,1,0:T(1,128)S(1)} all-to-all(s32[32,1,2176]{2,1,0:T(1,128)S(1)} %bitcast.6), channel_id=1, replica_groups=mesh['pair'=16,'slab'=2] {'pair','slab'}, dimensions={0} | all-to-all | bytes 557056 | tf_op jit(solution)/shard_map/all_to_all | solution.py:289
  32.0 0.7 %total.1 = bf16[2,16,16,128]{3,2,1,0:T(8,128)(2,1)} custom-call(s32[544,128]{1,0:T(8,128)S(1)} %bitcast.7), custom_call_target="tpu_custom_call" | custom-call | tf_op jit(solution)/shard_map/total/pallas_call | solution.py:293
Async XLA Ops:
  1.8 15.9 %all-to-all-start = ((bf16[32,8,256]{2,1,0:T(8,128)(2,1)}), bf16[32,8,256]{2,1,0:T(8,128)(2,1)S(1)}, u32[]{:S(2)}, u32[]{:S(2)}) async-start(bf16[32,8,256]{2,1,0:T(8,128)(2,1)} %bitcast.12), calls=%async_computation | async-start | bytes 262144 | tf_op jit(solution)/shard_map/all_to_all | solution.py:246
  9.1 0.7 %copy-start = (s32[1,16,16]{2,1,0:T(8,128)S(1)}, s32[1,16,16]{2,1,0:T(8,128)}, u32[]{:S(2)}) copy-start(s32[1,16,16]{2,1,0:T(8,128)} %screen_hbm.1) | copy-start | bytes 3076
  9.8 0.7 %copy-start.1 = (s32[256]{0:T(256)S(1)}, s32[256]{0:T(256)}, u32[]{:S(2)}) copy-start(s32[256]{0:T(256)} %param.8) | copy-start | bytes 3076
  10.5 0.7 %copy-start.2 = (s32[256]{0:T(256)S(1)}, s32[256]{0:T(256)}, u32[]{:S(2)}) copy-start(s32[256]{0:T(256)} %param.6) | copy-start | bytes 3076

commit v4 on v3

--- a/solution.py
+++ b/solution.py
@@ -14,20 +14,20 @@
 RESIDENT = 13 << 18
 
 
-def tile_places(owner_ref, owners, per_owner):
-    pieces = owner_ref.shape[0]
-    tiles = pieces * LANES
-    rows = lax.broadcasted_iota(jnp.int32, (owners, LANES), 0)
-    held = jnp.concatenate(
-        [(owner_ref[j : j + 1, :] == rows).astype(jnp.float32) for j in range(pieces)], axis=1
-    )
-    earlier = (
+def earlier_tiles(tiles):
+    return (
         lax.broadcasted_iota(jnp.int32, (tiles, tiles), 0)
         < lax.broadcasted_iota(jnp.int32, (tiles, tiles), 1)
     ).astype(jnp.bfloat16)
-    rank = jnp.dot(held.astype(jnp.bfloat16), earlier, preferred_element_type=jnp.float32)
-    first = lax.broadcasted_iota(jnp.int32, (owners, tiles), 0).astype(jnp.float32) * per_owner
-    return jnp.sum(held * (first + rank), axis=0, keepdims=True)
+
+
+def tile_ranks(owner_ref, owners, earlier):
+    rows = lax.broadcasted_iota(jnp.int32, (owners, LANES), 0)
+    held = jnp.concatenate(
+        [(owner_ref[j : j + 1, :] == rows).astype(jnp.float32) for j in range(owner_ref.shape[0])],
+        axis=1,
+    )
+    return held, jnp.dot(held.astype(jnp.bfloat16), earlier, preferred_element_type=jnp.float32)
 
 
 def fetch(source, target, sem):
@@ -36,14 +36,19 @@
     return copy
 
 
-def order_kernel(owners, owner_hbm, amps_hbm, out_ref, owner_ref, amps_ref, sems):
+def order_kernel(owners, slabs, owner_hbm, amps_hbm, out_ref, owner_ref, amps_ref, sems):
     local_rows, tiles, width = amps_ref.shape
+    tiles_here = tiles // (owners * slabs)
     owner_copy = fetch(owner_hbm, owner_ref, sems.at[0])
     amps_copy = fetch(amps_hbm, amps_ref, sems.at[1])
+    earlier = earlier_tiles(tiles)
+    rows = lax.broadcasted_iota(jnp.int32, (tiles, tiles), 0).astype(jnp.float32)
+    first = lax.broadcasted_iota(jnp.int32, (owners, tiles), 0).astype(jnp.float32) * tiles_here
     owner_copy.wait()
-    place = tile_places(owner_ref, owners, tiles // owners)
-    rows = lax.broadcasted_iota(jnp.int32, (tiles, tiles), 0).astype(jnp.float32)
-    pick = (rows == place).astype(jnp.bfloat16)
+    held, rank = tile_ranks(owner_ref, owners, earlier)
+    slab = jnp.floor((rank + 0.5) * (1.0 / tiles_here))
+    place = first + rank + slab * ((owners - 1) * tiles_here)
+    pick = (rows == jnp.sum(held * place, axis=0, keepdims=True)).astype(jnp.bfloat16)
     amps_copy.wait()
     for i in range(local_rows):
         out_ref[:, i * width : (i + 1) * width] = jnp.dot(
@@ -80,14 +85,16 @@
         fetch(block_hbm.at[0, rows, 0:kept], out_ref.at[rows, :], block_sems.at[k])
         for k, rows in enumerate(spans)
     ]
+    pieces = owner_ref.shape[0]
+    tiles = pieces * LANES
+    earlier = earlier_tiles(tiles)
     for copy in small:
         copy.wait()
-    pieces = owner_ref.shape[0]
-    tiles = pieces * LANES
-    place = tile_places(owner_ref, owners, per_owner)
-    first = lax.axis_index("pair") * per_owner
-    rows = (lax.broadcasted_iota(jnp.int32, (per_owner, tiles), 0) + first).astype(jnp.float32)
-    mine = (rows == place).astype(jnp.bfloat16)
+    held, rank = tile_ranks(owner_ref, owners, earlier)
+    here = lax.broadcasted_iota(jnp.int32, (owners, tiles), 0) == lax.axis_index("pair")
+    rank = jnp.sum(jnp.where(here, held * (rank + 1.0), 0.0), axis=0, keepdims=True) - 1.0
+    rows = lax.broadcasted_iota(jnp.int32, (per_owner, tiles), 0).astype(jnp.float32)
+    mine = (rows == rank).astype(jnp.bfloat16)
     classes = lax.broadcasted_iota(jnp.int32, (16, LANES), 0)
     kinds = jnp.concatenate(
         [(symmetry_ref[j : j + 1, :] == classes).astype(jnp.float32) for j in range(pieces)],
@@ -198,7 +205,7 @@
     for owner in range(owners):
         totals = [0.0, 0.0]
         for slab in range(slabs):
-            source = owner * slabs + slab
+            source = slab * owners + owner
             values = halves(coded_ref[source * pitch : source * pitch + per_owner, :])
             for i in range(2):
                 totals[i] = totals[i] + values[i] * grains[i][source : source + 1, :]
@@ -211,6 +218,10 @@
         copy.wait()
 
 
+def pinned(array):
+    return pltpu.with_memory_space_constraint(array, pltpu.HBM)
+
+
 def on_device(amps, symmetry, screen, owner, integrals):
     owners, slabs = lax.axis_size("pair"), lax.axis_size("slab")
     devices = owners * slabs
@@ -218,20 +229,19 @@
     per_owner = tiles // owners
     tiles_here = per_owner // slabs
     rows_here, columns = integrals.shape[1:]
-    everyone = ("pair", "slab")
+    everyone = ("slab", "pair")
     owner = owner.reshape(-1, LANES)
     symmetry = symmetry.reshape(-1, LANES)
     in_vmem = pl.BlockSpec(memory_space=pltpu.VMEM)
-    in_hbm = pl.BlockSpec(memory_space=pl.ANY)
+    in_hbm = pl.BlockSpec(memory_space=pltpu.HBM)
     dma = pltpu.SemaphoreType.DMA
-    alone = pltpu.CompilerParams(vmem_limit_bytes=60 << 20)
     beside = pltpu.CompilerParams(vmem_limit_bytes=48 << 20)
     small = pltpu.CompilerParams(vmem_limit_bytes=16 << 20)
     kept = min(columns, RESIDENT // (rows_here * integrals.dtype.itemsize) // width * width)
     rest = max(columns - kept, 2 * width)
 
     ordered = pl.pallas_call(
-        functools.partial(order_kernel, owners),
+        functools.partial(order_kernel, owners, slabs),
         out_shape=jax.ShapeDtypeStruct((tiles, local_rows * width), amps.dtype),
         in_specs=[in_hbm, in_hbm],
         out_specs=in_vmem,
@@ -240,9 +250,9 @@
             pltpu.VMEM(amps.shape, amps.dtype),
             dma((2,)),
         ],
-        compiler_params=alone,
+        compiler_params=beside,
         name="order_amps",
-    )(owner, amps)
+    )(pinned(owner), pinned(amps))
     arrived = lax.all_to_all(
         ordered.reshape(devices, tiles_here, local_rows * width), everyone, 0, 0, tiled=True
     ).reshape(devices * tiles_here, local_rows * width)
@@ -268,7 +278,7 @@
             flops=rows_here * columns, bytes_accessed=4 * rows_here * columns, transcendentals=0
         ),
         name="mask_block",
-    )(owner, symmetry, screen, integrals)
+    )(pinned(owner), pinned(symmetry), pinned(screen), pinned(integrals))
 
     pitch = per_owner + 1
     coded = pl.pallas_call(
@@ -285,7 +295,7 @@
         ],
         compiler_params=beside,
         name="partial_sums",
-    )(arrived, allowed, masked, integrals)
+    )(arrived, allowed, masked, pinned(integrals))
     returned = lax.all_to_all(
         coded.reshape(devices, 1, pitch * width), everyone, 0, 0, tiled=True
     ).reshape(devices * pitch, width)

time: 33.1 us -> 32.4 us (0.979)
  local copies, waits for them, and re-layouts: 2.05 us -> 0 us
  waiting for transfers between devices: 4.52 us -> 5.64 us
  Pallas kernels: 6.2 us -> 6.74 us
    unnamed x6 -> x0, local copies, waits for them, and re-layouts: 2.05 us -> none
    all_to_all x1, waiting for transfers between devices: 4.52 us -> 5.64 us  [on_device(): lax.all_to_all(ordered.reshape(devices, tiles_here, local_rows * width),...]
    pallas_call x1, Pallas kernels: 2.04 us -> 2.58 us  [on_device(): pl.pallas_call(functools.partial(mask_kernel, owners), out_shape=(pltpu.V...]
  transfers between devices with their start and end apart: 1 -> 1, of which waited for: 1 -> 1; matrix products, arithmetic and copies ran while one was open for 0% -> 0% of each run, Pallas kernels for 6% -> 8%
where the time goes in v4:
time: 32.4 us; the launch traced here: 32.1 us
  blocking collectives  12.4 us (38%)
  starting transfers between devices  7.3 us (23%)
  Pallas kernels  6.74 us (21%)
  waiting for transfers between devices  5.64 us (17%)
    all_to_all x1, blocking collectives, on_device(): lax.all_to_all(coded.reshape(devices, 1, pitch * width), everyone, 0, 0,...  12.4 us
    all_to_all x1, starting transfers between devices, on_device(): lax.all_to_all(ordered.reshape(devices, tiles_here, local_rows * width),...  7.3 us
    all_to_all x1, waiting for transfers between devices, on_device(): lax.all_to_all(ordered.reshape(devices, tiles_here, local_rows * width),...  5.64 us
    pallas_call x1, Pallas kernels, on_device(): pl.pallas_call(functools.partial(mask_kernel, owners), out_shape=(pltpu.V...  2.58 us
    pallas_call x1, Pallas kernels, on_device(): pl.pallas_call(functools.partial(order_kernel, owners, slabs), out_shape=...  1.82 us
    pallas_call x1, Pallas kernels, on_device(): pl.pallas_call(functools.partial(partial_kernel, devices, local_rows), ou...  1.6 us
    pallas_call x1, Pallas kernels, on_device(): pl.pallas_call(functools.partial(total_kernel, slabs), out_shape=jax.Shap...  0.74 us
  transfers between devices with their start and end apart: 1, of which 1 were waited for; matrix products, arithmetic and copies ran while one was open for 0% of the time, Pallas kernels for 8%

profile of v4, /device:TPU:0, one launch (start us, length us, event | category | flops | bytes accessed | tf_op | source)
XLA Modules:
  0.0 32.1 jit_solution(8859851443464683887)
XLA Ops:
  0.0 1.8 %order_amps.1 = bf16[256,256]{1,0:T(8,128)(2,1)} custom-call(s32[2,128]{1,0:T(2,128)} %bitcast.9, bf16[2,256,128]{2,1,0:T(8,128)(2,1)} %amps_hbm.1), custom_call_target="tpu_custom_call" | custom-call | tf_op jit(solution)/shard_map/order_amps/pallas_call | solution.py:243
  1.8 7.3 %all-to-all-start = ((bf16[32,8,256]{2,1,0:T(8,128)(2,1)}), bf16[32,8,256]{2,1,0:T(8,128)(2,1)S(1)}, u32[]{:S(2)}, u32[]{:S(2)}) async-start(bf16[32,8,256]{2,1,0:T(8,128)(2,1)} %bitcast.1), calls=%async_computation | async-start | bytes 262144 | tf_op jit(solution)/shard_map/all_to_all | solution.py:256
  9.1 2.6 %mask_block.1 = (f32[8,384]{1,0:T(8,128)S(1)}, bf16[1024,1664]{1,0:T(8,128)(2,1)S(1)}) custom-call(s32[2,128]{1,0:T(2,128)} %bitcast.10, s32[2,128]{1,0:T(2,128)} %bitcast.11, s32[1,16,16]{2,1,0:T(8,128)} %screen_hbm.1, bf16[1,1024,2048]{2,1,0:T(8,128)(2,1)} %block_hbm.3), custom_call_target="tpu_custom_call" | custom-call | flops 2097152 | bytes 8388608 | tf_op jit(solution)/shard_map/mask_block/pallas_call | solution.py:260
  11.7 5.6 %all-to-all-done = bf16[32,8,256]{2,1,0:T(8,128)(2,1)S(1)} async-done(((bf16[32,8,256]{2,1,0:T(8,128)(2,1)}), bf16[32,8,256]{2,1,0:T(8,128)(2,1)S(1)}, u32[]{:S(2)}, u32[]{:S(2)}) %all-to-all-start) | async-done | bytes 131104 | tf_op jit(solution)/shard_map/all_to_all | solution.py:256
  17.4 1.6 %partial_sums.1 = s32[544,128]{1,0:T(8,128)S(1)} custom-call(bf16[256,256]{1,0:T(8,128)(2,1)S(1)} %bitcast.8, f32[8,384]{1,0:T(8,128)S(1)} %get-tuple-element.7.allowed_ref, bf16[1024,1664]{1,0:T(8,128)(2,1)S(1)} %get-tuple-element.8.masked_ref, bf16[1,1024,2048]{2,1,0:T(8,128)(2,1)} %block_hbm.3), custom_call_target="tpu_custom_call" | custom-call | tf_op jit(solution)/shard_map/partial_sums/pallas_call | solution.py:284
  19.0 12.4 %all_to_all.10 = s32[32,1,2176]{2,1,0:T(1,128)S(1)} all-to-all(s32[32,1,2176]{2,1,0:T(1,128)S(1)} %bitcast.6), channel_id=1, replica_groups=mesh['pair'=16,'slab'=2] {'slab','pair'}, dimensions={0} | all-to-all | bytes 557056 | tf_op jit(solution)/shard_map/all_to_all | solution.py:299
  31.4 0.7 %total.1 = bf16[2,16,16,128]{3,2,1,0:T(8,128)(2,1)} custom-call(s32[544,128]{1,0:T(8,128)S(1)} %bitcast.7), custom_call_target="tpu_custom_call" | custom-call | tf_op jit(solution)/shard_map/total/pallas_call | solution.py:303
Async XLA Ops:
  1.8 15.5 %all-to-all-start = ((bf16[32,8,256]{2,1,0:T(8,128)(2,1)}), bf16[32,8,256]{2,1,0:T(8,128)(2,1)S(1)}, u32[]{:S(2)}, u32[]{:S(2)}) async-start(bf16[32,8,256]{2,1,0:T(8,128)(2,1)} %bitcast.1), calls=%async_computation | async-start | bytes 262144 | tf_op jit(solution)/shard_map/all_to_all | solution.py:256

commit v5 on v4

--- a/solution.py
+++ b/solution.py
@@ -2,6 +2,7 @@
 
 import jax
 import jax.numpy as jnp
+import numpy as np
 from jax import lax
 from jax.experimental import pallas as pl
 from jax.experimental.pallas import tpu as pltpu
@@ -9,9 +10,16 @@
 
 LANES = 128
 CODE_MAX = 32767.0
+BIAS = 32768.0
 SCALE_STEPS = 128.0
-LEAST = 1e-37
+LEAST = 1e-33
+ORDER_SEED = 22
 RESIDENT = 13 << 18
+
+
+def exchange_order(devices):
+    order = np.random.RandomState(ORDER_SEED).permutation(devices)
+    return [int(device) for device in order], [int(place) for place in np.argsort(order)]
 
 
 def earlier_tiles(tiles):
@@ -36,24 +44,36 @@
     return copy
 
 
-def order_kernel(owners, slabs, owner_hbm, amps_hbm, out_ref, owner_ref, amps_ref, sems):
-    local_rows, tiles, width = amps_ref.shape
+def order_kernel(owners, slabs, places, owner_hbm, amps_hbm, out_ref, owner_ref, amps_ref, sems):
+    local_rows, tiles, width = amps_hbm.shape
     tiles_here = tiles // (owners * slabs)
     owner_copy = fetch(owner_hbm, owner_ref, sems.at[0])
-    amps_copy = fetch(amps_hbm, amps_ref, sems.at[1])
+    amps_copies = [
+        fetch(amps_hbm.at[i], amps_ref.at[:, i * width : (i + 1) * width], sems.at[1 + i])
+        for i in range(local_rows)
+    ]
     earlier = earlier_tiles(tiles)
     rows = lax.broadcasted_iota(jnp.int32, (tiles, tiles), 0).astype(jnp.float32)
-    first = lax.broadcasted_iota(jnp.int32, (owners, tiles), 0).astype(jnp.float32) * tiles_here
+    holder = lax.broadcasted_iota(jnp.int32, (owners, LANES), 0)
+    bases = []
+    for index in range(slabs):
+        base = jnp.zeros((owners, LANES), jnp.float32)
+        for device in range(owners):
+            entry = (places[index * owners + device] - index) * tiles_here
+            base = jnp.where(holder == device, float(entry), base)
+        bases.append(jnp.concatenate([base] * (tiles // LANES), axis=1))
     owner_copy.wait()
     held, rank = tile_ranks(owner_ref, owners, earlier)
     slab = jnp.floor((rank + 0.5) * (1.0 / tiles_here))
-    place = first + rank + slab * ((owners - 1) * tiles_here)
+    place = rank
+    for index, base in enumerate(bases):
+        place = place + jnp.where(slab == index, base, 0.0)
     pick = (rows == jnp.sum(held * place, axis=0, keepdims=True)).astype(jnp.bfloat16)
-    amps_copy.wait()
-    for i in range(local_rows):
-        out_ref[:, i * width : (i + 1) * width] = jnp.dot(
-            pick, amps_ref[i], preferred_element_type=jnp.float32
-        ).astype(out_ref.dtype)
+    for copy in amps_copies:
+        copy.wait()
+    out_ref[...] = jnp.dot(pick, amps_ref[...], preferred_element_type=jnp.float32).astype(
+        out_ref.dtype
+    )
 
 
 def mask_kernel(
@@ -177,25 +197,25 @@
     code = jnp.ceil(jnp.log2(top) * SCALE_STEPS) + 1.0
     grain = jnp.exp2(code * (-1.0 / SCALE_STEPS)) * CODE_MAX
 
-    def pack(words):
-        return (words[devices:] << 16) | (words[:devices] & 0xFFFF)
-
-    out_ref[pl.ds(per_owner, devices, stride=pitch), :] = pack(code.astype(jnp.int32))
+    def pack(value):
+        words = (value + (BIAS + 0.5)).astype(jnp.int32)
+        return (words[devices:] << 16) | words[:devices]
+
+    out_ref[pl.ds(per_owner, devices, stride=pitch), :] = pack(code)
     for tile in range(per_owner):
         value = sums[:, tile * width : (tile + 1) * width]
-        out_ref[pl.ds(tile, devices, stride=pitch), :] = pack(
-            jnp.floor(value * grain + 0.5).astype(jnp.int32)
-        )
-
-
-def total_kernel(slabs, coded_ref, out_hbm, out_ref, sems):
+        out_ref[pl.ds(tile, devices, stride=pitch), :] = pack(value * grain)
+
+
+def total_kernel(slabs, places, coded_ref, out_hbm, out_ref, sems):
     local_rows, owners, per_owner, width = out_ref.shape
     devices = owners * slabs
     pitch = per_owner + 1
     scales = coded_ref[pl.ds(per_owner, devices, stride=pitch), :]
 
     def halves(words):
-        return ((words << 16) >> 16).astype(jnp.float32), (words >> 16).astype(jnp.float32)
+        low, high = words & 0xFFFF, lax.shift_right_logical(words, 16)
+        return low.astype(jnp.float32) - BIAS, high.astype(jnp.float32) - BIAS
 
     grains = [
         jnp.exp2(code * (1.0 / SCALE_STEPS)) * (1.0 / CODE_MAX) for code in halves(scales)
@@ -205,7 +225,7 @@
     for owner in range(owners):
         totals = [0.0, 0.0]
         for slab in range(slabs):
-            source = slab * owners + owner
+            source = places[slab * owners + owner]
             values = halves(coded_ref[source * pitch : source * pitch + per_owner, :])
             for i in range(2):
                 totals[i] = totals[i] + values[i] * grains[i][source : source + 1, :]
@@ -230,6 +250,7 @@
     tiles_here = per_owner // slabs
     rows_here, columns = integrals.shape[1:]
     everyone = ("slab", "pair")
+    order, places = exchange_order(devices)
     owner = owner.reshape(-1, LANES)
     symmetry = symmetry.reshape(-1, LANES)
     in_vmem = pl.BlockSpec(memory_space=pltpu.VMEM)
@@ -241,20 +262,20 @@
     rest = max(columns - kept, 2 * width)
 
     ordered = pl.pallas_call(
-        functools.partial(order_kernel, owners, slabs),
+        functools.partial(order_kernel, owners, slabs, places),
         out_shape=jax.ShapeDtypeStruct((tiles, local_rows * width), amps.dtype),
-        in_specs=[in_hbm, in_hbm],
+        in_specs=[in_hbm] * 2,
         out_specs=in_vmem,
         scratch_shapes=[
             pltpu.VMEM(owner.shape, owner.dtype),
-            pltpu.VMEM(amps.shape, amps.dtype),
-            dma((2,)),
+            pltpu.VMEM((tiles, local_rows * width), amps.dtype),
+            dma((1 + local_rows,)),
         ],
         compiler_params=beside,
         name="order_amps",
     )(pinned(owner), pinned(amps))
     arrived = lax.all_to_all(
-        ordered.reshape(devices, tiles_here, local_rows * width), everyone, 0, 0, tiled=True
+        ordered.reshape(devices, tiles_here, local_rows * width), everyone, 0, 0, tiled=True, axis_index_groups=[order]
     ).reshape(devices * tiles_here, local_rows * width)
 
     allowed, masked = pl.pallas_call(
@@ -297,11 +318,11 @@
         name="partial_sums",
     )(arrived, allowed, masked, pinned(integrals))
     returned = lax.all_to_all(
-        coded.reshape(devices, 1, pitch * width), everyone, 0, 0, tiled=True
+        coded.reshape(devices, 1, pitch * width), everyone, 0, 0, tiled=True, axis_index_groups=[order]
     ).reshape(devices * pitch, width)
 
     return pl.pallas_call(
-        functools.partial(total_kernel, slabs),
+        functools.partial(total_kernel, slabs, places),
         out_shape=jax.ShapeDtypeStruct((local_rows, owners, per_owner, width), amps.dtype),
         in_specs=[in_vmem],
         out_specs=in_hbm,

time: 32.4 us -> 31.3 us (0.966)
  waiting for transfers between devices: 5.64 us -> 5.08 us
  blocking collectives: 12.4 us -> 11.9 us
    all_to_all x1, waiting for transfers between devices: 5.64 us -> 5.08 us  [on_device(): lax.all_to_all(ordered.reshape(devices, tiles_here, local_rows * width),...]
    all_to_all x1, blocking collectives: 12.4 us -> 11.9 us  [on_device(): lax.all_to_all(coded.reshape(devices, 1, pitch * width), everyone, 0, 0,...]
where the time goes in v5:
time: 31.3 us; the launch traced here: 30.9 us
  blocking collectives  11.9 us (38%)
  starting transfers between devices  7.3 us (23%)
  Pallas kernels  6.67 us (21%)
  waiting for transfers between devices  5.08 us (16%)
    all_to_all x1, blocking collectives, on_device(): lax.all_to_all(coded.reshape(devices, 1, pitch * width), everyone, 0, 0,...  11.9 us
    all_to_all x1, starting transfers between devices, on_device(): lax.all_to_all(ordered.reshape(devices, tiles_here, local_rows * width),...  7.3 us
    all_to_all x1, waiting for transfers between devices, on_device(): lax.all_to_all(ordered.reshape(devices, tiles_here, local_rows * width),...  5.08 us
    pallas_call x1, Pallas kernels, on_device(): pl.pallas_call(functools.partial(mask_kernel, owners), out_shape=(pltpu.V...  2.58 us
    pallas_call x1, Pallas kernels, on_device(): pl.pallas_call(functools.partial(order_kernel, owners, slabs, places), ou...  1.77 us
    pallas_call x1, Pallas kernels, on_device(): pl.pallas_call(functools.partial(partial_kernel, devices, local_rows), ou...  1.57 us
    pallas_call x1, Pallas kernels, on_device(): pl.pallas_call(functools.partial(total_kernel, slabs, places), out_shape=...  0.75 us
  transfers between devices with their start and end apart: 1, of which 1 were waited for; matrix products, arithmetic and copies ran while one was open for 0% of the time, Pallas kernels for 8%

profile of v5, /device:TPU:0, one launch (start us, length us, event | category | flops | bytes accessed | tf_op | source)
XLA Modules:
  0.0 30.9 jit_solution(12405933502904237875)
XLA Ops:
  0.0 1.8 %order_amps.1 = bf16[256,256]{1,0:T(8,128)(2,1)} custom-call(s32[2,128]{1,0:T(2,128)} %bitcast.9, bf16[2,256,128]{2,1,0:T(8,128)(2,1)} %amps_hbm.1), custom_call_target="tpu_custom_call" | custom-call | tf_op jit(solution)/shard_map/order_amps/pallas_call | solution.py:264
  1.8 7.3 %all-to-all-start = ((bf16[32,8,256]{2,1,0:T(8,128)(2,1)}), bf16[32,8,256]{2,1,0:T(8,128)(2,1)S(1)}, u32[]{:S(2)}, u32[]{:S(2)}) async-start(bf16[32,8,256]{2,1,0:T(8,128)(2,1)} %bitcast.1), calls=%async_computation | async-start | bytes 262144 | tf_op jit(solution)/shard_map/all_to_all | solution.py:277
  9.1 2.6 %mask_block.1 = (f32[8,384]{1,0:T(8,128)S(1)}, bf16[1024,1664]{1,0:T(8,128)(2,1)S(1)}) custom-call(s32[2,128]{1,0:T(2,128)} %bitcast.10, s32[2,128]{1,0:T(2,128)} %bitcast.11, s32[1,16,16]{2,1,0:T(8,128)} %screen_hbm.1, bf16[1,1024,2048]{2,1,0:T(8,128)(2,1)} %block_hbm.3), custom_call_target="tpu_custom_call" | custom-call | flops 2097152 | bytes 8388608 | tf_op jit(solution)/shard_map/mask_block/pallas_call | solution.py:281
  11.7 5.1 %all-to-all-done = bf16[32,8,256]{2,1,0:T(8,128)(2,1)S(1)} async-done(((bf16[32,8,256]{2,1,0:T(8,128)(2,1)}), bf16[32,8,256]{2,1,0:T(8,128)(2,1)S(1)}, u32[]{:S(2)}, u32[]{:S(2)}) %all-to-all-start) | async-done | bytes 131104 | tf_op jit(solution)/shard_map/all_to_all | solution.py:277
  16.8 1.6 %partial_sums.1 = s32[544,128]{1,0:T(8,128)S(1)} custom-call(bf16[256,256]{1,0:T(8,128)(2,1)S(1)} %bitcast.8, f32[8,384]{1,0:T(8,128)S(1)} %get-tuple-element.7.allowed_ref, bf16[1024,1664]{1,0:T(8,128)(2,1)S(1)} %get-tuple-element.8.masked_ref, bf16[1,1024,2048]{2,1,0:T(8,128)(2,1)} %block_hbm.3), custom_call_target="tpu_custom_call" | custom-call | tf_op jit(solution)/shard_map/partial_sums/pallas_call | solution.py:305
  18.3 11.9 %all_to_all.10 = s32[32,1,2176]{2,1,0:T(1,128)S(1)} all-to-all(s32[32,1,2176]{2,1,0:T(1,128)S(1)} %bitcast.6), channel_id=1, replica_groups={{25,27,15,20,6,3,21,2,30,1,31,17,10,7,19,18,4,14,26,28,5,23,16,9,22,13,..., dimensions={0} | all-to-all | bytes 557056 | tf_op jit(solution)/shard_map/all_to_all | solution.py:320
  30.2 0.7 %total.1 = bf16[2,16,16,128]{3,2,1,0:T(8,128)(2,1)} custom-call(s32[544,128]{1,0:T(8,128)S(1)} %bitcast.7), custom_call_target="tpu_custom_call" | custom-call | tf_op jit(solution)/shard_map/total/pallas_call | solution.py:324
Async XLA Ops:
  1.8 15.0 %all-to-all-start = ((bf16[32,8,256]{2,1,0:T(8,128)(2,1)}), bf16[32,8,256]{2,1,0:T(8,128)(2,1)S(1)}, u32[]{:S(2)}, u32[]{:S(2)}) async-start(bf16[32,8,256]{2,1,0:T(8,128)(2,1)} %bitcast.1), calls=%async_computation | async-start | bytes 262144 | tf_op jit(solution)/shard_map/all_to_all | solution.py:277

commit v6 on v5

--- a/solution.py
+++ b/solution.py
@@ -44,7 +44,9 @@
     return copy
 
 
-def order_kernel(owners, slabs, places, owner_hbm, amps_hbm, out_ref, owner_ref, amps_ref, sems):
+def order_kernel(
+    owners, slabs, places, owner_hbm, amps_hbm, out_hbm, owner_ref, amps_ref, out_ref, sems, out_sems
+):
     local_rows, tiles, width = amps_hbm.shape
     tiles_here = tiles // (owners * slabs)
     owner_copy = fetch(owner_hbm, owner_ref, sems.at[0])
@@ -71,9 +73,15 @@
     pick = (rows == jnp.sum(held * place, axis=0, keepdims=True)).astype(jnp.bfloat16)
     for copy in amps_copies:
         copy.wait()
-    out_ref[...] = jnp.dot(pick, amps_ref[...], preferred_element_type=jnp.float32).astype(
-        out_ref.dtype
-    )
+    copies = []
+    for part in range(2):
+        rows = slice(part * tiles // 2, (part + 1) * tiles // 2)
+        out_ref[rows, :] = jnp.dot(
+            pick[rows], amps_ref[...], preferred_element_type=jnp.float32
+        ).astype(out_ref.dtype)
+        copies.append(fetch(out_ref.at[rows, :], out_hbm.at[rows, :], out_sems.at[part]))
+    for copy in copies:
+        copy.wait()
 
 
 def mask_kernel(
@@ -265,11 +273,13 @@
         functools.partial(order_kernel, owners, slabs, places),
         out_shape=jax.ShapeDtypeStruct((tiles, local_rows * width), amps.dtype),
         in_specs=[in_hbm] * 2,
-        out_specs=in_vmem,
+        out_specs=in_hbm,
         scratch_shapes=[
             pltpu.VMEM(owner.shape, owner.dtype),
             pltpu.VMEM((tiles, local_rows * width), amps.dtype),
+            pltpu.VMEM((tiles, local_rows * width), amps.dtype),
             dma((1 + local_rows,)),
+            dma((2,)),
         ],
         compiler_params=beside,
         name="order_amps",

time: 31.3 us -> 31.3 us (level)
  no operation moved by 1% of the time
where the time goes in v6:
time: 31.3 us; the launch traced here: 30.9 us
  blocking collectives  11.9 us (38%)
  starting transfers between devices  7.3 us (23%)
  Pallas kernels  6.67 us (21%)
  waiting for transfers between devices  5.08 us (16%)
    all_to_all x1, blocking collectives, on_device(): lax.all_to_all(coded.reshape(devices, 1, pitch * width), everyone, 0, 0,...  11.9 us
    all_to_all x1, starting transfers between devices, on_device(): lax.all_to_all(ordered.reshape(devices, tiles_here, local_rows * width),...  7.3 us
    all_to_all x1, waiting for transfers between devices, on_device(): lax.all_to_all(ordered.reshape(devices, tiles_here, local_rows * width),...  5.08 us
    pallas_call x1, Pallas kernels, on_device(): pl.pallas_call(functools.partial(mask_kernel, owners), out_shape=(pltpu.V...  2.58 us
    pallas_call x1, Pallas kernels, on_device(): pl.pallas_call(functools.partial(order_kernel, owners, slabs, places), ou...  1.77 us
    pallas_call x1, Pallas kernels, on_device(): pl.pallas_call(functools.partial(partial_kernel, devices, local_rows), ou...  1.57 us
    pallas_call x1, Pallas kernels, on_device(): pl.pallas_call(functools.partial(total_kernel, slabs, places), out_shape=...  0.75 us
  transfers between devices with their start and end apart: 1, of which 1 were waited for; matrix products, arithmetic and copies ran while one was open for 0% of the time, Pallas kernels for 8%

profile of v6, /device:TPU:0, one launch (start us, length us, event | category | flops | bytes accessed | tf_op | source)
XLA Modules:
  0.0 30.9 jit_solution(94840632828436667)
XLA Ops:
  0.0 1.8 %order_amps.1 = bf16[256,256]{1,0:T(8,128)(2,1)} custom-call(s32[2,128]{1,0:T(2,128)} %bitcast.9, bf16[2,256,128]{2,1,0:T(8,128)(2,1)} %amps_hbm.1), custom_call_target="tpu_custom_call" | custom-call | tf_op jit(solution)/shard_map/order_amps/pallas_call | solution.py:272
  1.8 7.3 %all-to-all-start = ((bf16[32,8,256]{2,1,0:T(8,128)(2,1)}), bf16[32,8,256]{2,1,0:T(8,128)(2,1)S(1)}, u32[]{:S(2)}, u32[]{:S(2)}) async-start(bf16[32,8,256]{2,1,0:T(8,128)(2,1)} %bitcast.1), calls=%async_computation | async-start | bytes 262144 | tf_op jit(solution)/shard_map/all_to_all | solution.py:287
  9.1 2.6 %mask_block.1 = (f32[8,384]{1,0:T(8,128)S(1)}, bf16[1024,1664]{1,0:T(8,128)(2,1)S(1)}) custom-call(s32[2,128]{1,0:T(2,128)} %bitcast.10, s32[2,128]{1,0:T(2,128)} %bitcast.11, s32[1,16,16]{2,1,0:T(8,128)} %screen_hbm.1, bf16[1,1024,2048]{2,1,0:T(8,128)(2,1)} %block_hbm.3), custom_call_target="tpu_custom_call" | custom-call | flops 2097152 | bytes 8388608 | tf_op jit(solution)/shard_map/mask_block/pallas_call | solution.py:291
  11.7 5.1 %all-to-all-done = bf16[32,8,256]{2,1,0:T(8,128)(2,1)S(1)} async-done(((bf16[32,8,256]{2,1,0:T(8,128)(2,1)}), bf16[32,8,256]{2,1,0:T(8,128)(2,1)S(1)}, u32[]{:S(2)}, u32[]{:S(2)}) %all-to-all-start) | async-done | bytes 131104 | tf_op jit(solution)/shard_map/all_to_all | solution.py:287
  16.8 1.6 %partial_sums.1 = s32[544,128]{1,0:T(8,128)S(1)} custom-call(bf16[256,256]{1,0:T(8,128)(2,1)S(1)} %bitcast.8, f32[8,384]{1,0:T(8,128)S(1)} %get-tuple-element.7.allowed_ref, bf16[1024,1664]{1,0:T(8,128)(2,1)S(1)} %get-tuple-element.8.masked_ref, bf16[1,1024,2048]{2,1,0:T(8,128)(2,1)} %block_hbm.3), custom_call_target="tpu_custom_call" | custom-call | tf_op jit(solution)/shard_map/partial_sums/pallas_call | solution.py:315
  18.3 11.9 %all_to_all.10 = s32[32,1,2176]{2,1,0:T(1,128)S(1)} all-to-all(s32[32,1,2176]{2,1,0:T(1,128)S(1)} %bitcast.6), channel_id=1, replica_groups={{25,27,15,20,6,3,21,2,30,1,31,17,10,7,19,18,4,14,26,28,5,23,16,9,22,13,..., dimensions={0} | all-to-all | bytes 557056 | tf_op jit(solution)/shard_map/all_to_all | solution.py:330
  30.2 0.7 %total.1 = bf16[2,16,16,128]{3,2,1,0:T(8,128)(2,1)} custom-call(s32[544,128]{1,0:T(8,128)S(1)} %bitcast.7), custom_call_target="tpu_custom_call" | custom-call | tf_op jit(solution)/shard_map/total/pallas_call | solution.py:334
Async XLA Ops:
  1.8 15.0 %all-to-all-start = ((bf16[32,8,256]{2,1,0:T(8,128)(2,1)}), bf16[32,8,256]{2,1,0:T(8,128)(2,1)S(1)}, u32[]{:S(2)}, u32[]{:S(2)}) async-start(bf16[32,8,256]{2,1,0:T(8,128)(2,1)} %bitcast.1), calls=%async_computation | async-start | bytes 262144 | tf_op jit(solution)/shard_map/all_to_all | solution.py:287

commit v7 on v5

--- a/solution.py
+++ b/solution.py
@@ -13,7 +13,7 @@
 BIAS = 32768.0
 SCALE_STEPS = 128.0
 LEAST = 1e-33
-ORDER_SEED = 22
+ORDER_SEED = 106
 RESIDENT = 13 << 18
 
 

time: 31.3 us -> 31.3 us (level)
  waiting for transfers between devices: 5.08 us -> 5.64 us
  blocking collectives: 11.9 us -> 11.4 us
    all_to_all x1, waiting for transfers between devices: 5.08 us -> 5.64 us  [on_device(): lax.all_to_all(ordered.reshape(devices, tiles_here, local_rows * width),...]
    all_to_all x1, blocking collectives: 11.9 us -> 11.4 us  [on_device(): lax.all_to_all(coded.reshape(devices, 1, pitch * width), everyone, 0, 0,...]
where the time goes in v7:
time: 31.3 us; the launch traced here: 31 us
  blocking collectives  11.4 us (36%)
  starting transfers between devices  7.3 us (23%)
  Pallas kernels  6.67 us (21%)
  waiting for transfers between devices  5.64 us (18%)
    all_to_all x1, blocking collectives, on_device(): lax.all_to_all(coded.reshape(devices, 1, pitch * width), everyone, 0, 0,...  11.4 us
    all_to_all x1, starting transfers between devices, on_device(): lax.all_to_all(ordered.reshape(devices, tiles_here, local_rows * width),...  7.3 us
    all_to_all x1, waiting for transfers between devices, on_device(): lax.all_to_all(ordered.reshape(devices, tiles_here, local_rows * width),...  5.64 us
    pallas_call x1, Pallas kernels, on_device(): pl.pallas_call(functools.partial(mask_kernel, owners), out_shape=(pltpu.V...  2.58 us
    pallas_call x1, Pallas kernels, on_device(): pl.pallas_call(functools.partial(order_kernel, owners, slabs, places), ou...  1.77 us
    pallas_call x1, Pallas kernels, on_device(): pl.pallas_call(functools.partial(partial_kernel, devices, local_rows), ou...  1.57 us
    pallas_call x1, Pallas kernels, on_device(): pl.pallas_call(functools.partial(total_kernel, slabs, places), out_shape=...  0.75 us
  transfers between devices with their start and end apart: 1, of which 1 were waited for; matrix products, arithmetic and copies ran while one was open for 0% of the time, Pallas kernels for 8%

profile of v7, /device:TPU:0, one launch (start us, length us, event | category | flops | bytes accessed | tf_op | source)
XLA Modules:
  0.0 31.0 jit_solution(8752997789501634303)
XLA Ops:
  0.0 1.8 %order_amps.1 = bf16[256,256]{1,0:T(8,128)(2,1)} custom-call(s32[2,128]{1,0:T(2,128)} %bitcast.9, bf16[2,256,128]{2,1,0:T(8,128)(2,1)} %amps_hbm.1), custom_call_target="tpu_custom_call" | custom-call | tf_op jit(solution)/shard_map/order_amps/pallas_call | solution.py:264
  1.8 7.3 %all-to-all-start = ((bf16[32,8,256]{2,1,0:T(8,128)(2,1)}), bf16[32,8,256]{2,1,0:T(8,128)(2,1)S(1)}, u32[]{:S(2)}, u32[]{:S(2)}) async-start(bf16[32,8,256]{2,1,0:T(8,128)(2,1)} %bitcast.1), calls=%async_computation | async-start | bytes 262144 | tf_op jit(solution)/shard_map/all_to_all | solution.py:277
  9.1 2.6 %mask_block.1 = (f32[8,384]{1,0:T(8,128)S(1)}, bf16[1024,1664]{1,0:T(8,128)(2,1)S(1)}) custom-call(s32[2,128]{1,0:T(2,128)} %bitcast.10, s32[2,128]{1,0:T(2,128)} %bitcast.11, s32[1,16,16]{2,1,0:T(8,128)} %screen_hbm.1, bf16[1,1024,2048]{2,1,0:T(8,128)(2,1)} %block_hbm.3), custom_call_target="tpu_custom_call" | custom-call | flops 2097152 | bytes 8388608 | tf_op jit(solution)/shard_map/mask_block/pallas_call | solution.py:281
  11.7 5.6 %all-to-all-done = bf16[32,8,256]{2,1,0:T(8,128)(2,1)S(1)} async-done(((bf16[32,8,256]{2,1,0:T(8,128)(2,1)}), bf16[32,8,256]{2,1,0:T(8,128)(2,1)S(1)}, u32[]{:S(2)}, u32[]{:S(2)}) %all-to-all-start) | async-done | bytes 131104 | tf_op jit(solution)/shard_map/all_to_all | solution.py:277
  17.3 1.6 %partial_sums.1 = s32[544,128]{1,0:T(8,128)S(1)} custom-call(bf16[256,256]{1,0:T(8,128)(2,1)S(1)} %bitcast.8, f32[8,384]{1,0:T(8,128)S(1)} %get-tuple-element.7.allowed_ref, bf16[1024,1664]{1,0:T(8,128)(2,1)S(1)} %get-tuple-element.8.masked_ref, bf16[1,1024,2048]{2,1,0:T(8,128)(2,1)} %block_hbm.3), custom_call_target="tpu_custom_call" | custom-call | tf_op jit(solution)/shard_map/partial_sums/pallas_call | solution.py:305
  18.9 11.4 %all_to_all.10 = s32[32,1,2176]{2,1,0:T(1,128)S(1)} all-to-all(s32[32,1,2176]{2,1,0:T(1,128)S(1)} %bitcast.6), channel_id=1, replica_groups={{3,25,30,29,16,0,22,31,15,27,8,18,12,13,10,2,6,24,1,26,5,4,11,17,7,20,2..., dimensions={0} | all-to-all | bytes 557056 | tf_op jit(solution)/shard_map/all_to_all | solution.py:320
  30.3 0.7 %total.1 = bf16[2,16,16,128]{3,2,1,0:T(8,128)(2,1)} custom-call(s32[544,128]{1,0:T(8,128)S(1)} %bitcast.7), custom_call_target="tpu_custom_call" | custom-call | tf_op jit(solution)/shard_map/total/pallas_call | solution.py:324
Async XLA Ops:
  1.8 15.5 %all-to-all-start = ((bf16[32,8,256]{2,1,0:T(8,128)(2,1)}), bf16[32,8,256]{2,1,0:T(8,128)(2,1)S(1)}, u32[]{:S(2)}, u32[]{:S(2)}) async-start(bf16[32,8,256]{2,1,0:T(8,128)(2,1)} %bitcast.1), calls=%async_computation | async-start | bytes 262144 | tf_op jit(solution)/shard_map/all_to_all | solution.py:277
